TPU v7x, 512 devices: a whole 4x4x16 slice. The times are simulated.
512 devices in a mesh: slab: 64 (over x_lo, z, core), pen: 8 (over x_hi, y).
Axes of the slice: x: 4 (x_hi: 2, x_lo: 2; x = x_hi * 2 + x_lo), y: 4, z: 16, core: 2. Of those that a mesh axis runs over, the one named last changes fastest.
Arguments:
- density: float32 [128, 256, 2048], P('slab', None, 'pen'), may hold values from -6 to 6
Outputs:
- coefficients: float32 [128, 256, 2048], P('slab', None, 'pen')
- approximation: float32 [64, 128, 1024], P('slab', None, 'pen')
All inputs are finite; a program needn't handle non-finite values.
Results may differ from a plain program's by a relative error of at most 0.00015.
Values sent between devices are 32-bit elements; how exact they have to be, the bound alone decides.
A program may use at most 128 MiB of HBM per device.

v0:
```python
import functools
import math

import jax
import jax.numpy as jnp
import ml_dtypes
import numpy as np
from jax import lax
from jax.experimental import pallas as pl
from jax.experimental.pallas import tpu as pltpu
from jax.sharding import PartitionSpec as P

MESH = pl.DeviceIdType.MESH
DECAY = math.log(2.0 + math.sqrt(3.0))
GROUP = 8
STATE_ROWS = 8
F32 = jnp.float32
BF16 = jnp.bfloat16


def inverse_mass(m):
    i = np.arange(m)[:, None]
    j = np.arange(m)[None, :]
    low, high = np.minimum(i, j), np.maximum(i, j)
    sign = np.where((high - low) % 2 == 0, 1.0, -1.0)
    ends = (1 - np.exp(-2 * (low + 1) * DECAY)) * (1 - np.exp(-2 * (m - high) * DECAY))
    scale = 3.0 / (2 * math.sqrt(3.0) * (1 - np.exp(-2 * (m + 1) * DECAY)))
    return scale * sign * np.exp(-(high - low) * DECAY) * ends


def refine_matrix(m):
    matrix = np.zeros((2 * m, m))
    j = np.arange(m)
    matrix[2 * j, j] = 1.0
    matrix[2 * j[:-1] + 1, j[:-1]] = 0.5
    matrix[2 * j[:-1] + 1, j[:-1] + 1] = 0.5
    matrix[2 * m - 1, m - 1] = 1.0
    return matrix


def project_matrix(m):
    j = np.arange(m)
    load = np.zeros((m, 2 * m + 2))
    w = np.where(j == m - 1, 1.0, 0.5)
    for offset, weight in ((-2, 0.5), (-1, 3.0), (0, 5.0), (1, 3.0), (2, 0.5)):
        keep = 2 * j + offset >= 0
        load[j[keep], 2 * j[keep] + offset] = weight / 6.0
    load[0, 0] = 4.5 / 6.0
    load[m - 1, 2 * m - 2] = (4.0 + w[-1] + 0.5) / 6.0
    load[m - 1, 2 * m - 1] = (1.0 + 4.0 * w[-1]) / 6.0
    return inverse_mass(m) @ load[:, : 2 * m]


def falling(m, i, start):
    d = i - start
    sign = np.where(d % 2 == 0, 1.0, -1.0)
    ends = (1 - np.exp(-2.0 * (m - i) * DECAY)) / (1 - np.exp(-2.0 * (m - start) * DECAY))
    return sign * np.exp(-d * DECAY) * ends


def rising(m, i, start):
    d = start - i
    sign = np.where(d % 2 == 0, 1.0, -1.0)
    ends = (1 - np.exp(-2.0 * (i + 1) * DECAY)) / (1 - np.exp(-2.0 * (start + 1) * DECAY))
    return sign * np.exp(-d * DECAY) * ends


class Blocks:
    def __init__(self, m, n):
        whole = project_matrix(m)
        size = m // n
        rows = np.arange(size)
        self.diagonal = np.stack(
            [whole[b * size : (b + 1) * size, 2 * b * size : 2 * (b + 1) * size] for b in range(n)]
        )
        self.to_later = np.zeros((n, 2 * size))
        self.to_earlier = np.zeros((n, 2 * size))
        self.later_first = np.zeros(n)
        self.earlier_last = np.zeros(n)
        self.falling = np.zeros((n, size))
        self.rising = np.zeros((n, size))
        self.from_earlier = np.zeros((n, n))
        self.from_later = np.zeros((n, n))
        inverse = inverse_mass(m)
        self.own_first = inverse[:size, 0]
        self.own_last = inverse[m - size :, m - 1]
        for b in range(n):
            columns = slice(2 * b * size, 2 * (b + 1) * size)
            first, last = b * size, (b + 1) * size - 1
            if b < n - 1:
                self.to_later[b] = whole[last + 1, columns]
            if b > 0:
                self.to_earlier[b] = whole[first - 1, columns]
            self.falling[b] = falling(m, first + rows, first)
            self.rising[b] = rising(m, first + rows, last)
            for c in range(n):
                if c < b:
                    self.from_earlier[b, c] = falling(m, first, (c + 1) * size)
                if c > b:
                    self.from_later[b, c] = rising(m, last, c * size - 1)
        self.first_to_later = inverse[size, 0] if n > 1 else 0.0
        self.last_to_earlier = inverse[m - size - 1, m - 1] if n > 1 else 0.0


def split(matrix):
    matrix = np.asarray(matrix, np.float32)
    high = matrix.astype(ml_dtypes.bfloat16)
    low = (matrix - high.astype(np.float32)).astype(ml_dtypes.bfloat16)
    return high, low


def parts(value):
    high = value.astype(BF16)
    return high, (value - high.astype(F32)).astype(BF16)


def dot(a, b, transposed=False):
    dims = (((1,), (1 if transposed else 0,)), ((), ()))
    return lax.dot_general(a, b, dims, preferred_element_type=F32)


def dot3(a, b, transposed=False):
    return (
        dot(a[0], b[0], transposed) + dot(a[0], b[1], transposed) + dot(a[1], b[0], transposed)
    )


class Scalars:
    def __init__(self, groups):
        g = GROUP
        self.local = 0
        self.to_later = self.local + 2 * g * g
        self.to_earlier = self.to_later + 2 * g
        self.falling = self.to_earlier + 2 * g
        self.rising = self.falling + g
        self.from_earlier = self.rising + g
        self.from_later = self.from_earlier + groups
        self.size = self.from_later + groups


def kernel(
    sizes,
    u_hbm, fixed_hbm, left_hbm, ends_hbm, table, pens,
    fine_hbm, coarse_hbm,
    u, fixed, left, ends, coarse_t, halo_in, halo_out, next_c, lift,
    out_a, in_a, out_b, in_b, out_c, in_c, out_x, in_x,
    fine, coarse,
    load_sem, store_sem,
    h1_send, h1_recv, h2_send, h2_recv,
    a_send, a_recv, b_send, b_recv, c_send, c_recv, x_send, x_recv,
):
    slabs, n_pen, groups, nx, nz, at = sizes
    part = nx // GROUP
    s = lax.axis_index("slab")
    p = lax.axis_index("pen")
    g = s // GROUP
    m = lax.rem(s, GROUP)

    loads = [
        pltpu.make_async_copy(u_hbm, u, load_sem.at[0]),
        pltpu.make_async_copy(fixed_hbm, fixed, load_sem.at[1]),
        pltpu.make_async_copy(left_hbm.at[p], left, load_sem.at[2]),
        pltpu.make_async_copy(ends_hbm.at[p], ends, load_sem.at[3]),
    ]
    for load in loads:
        load.start()

    members = [(g * GROUP + lax.rem(m + k, GROUP), p) for k in range(1, GROUP)]
    others = [(lax.rem(g + k, groups) * GROUP + m, p) for k in range(1, groups)]
    peers = [(s, lax.rem(p + k, n_pen)) for k in range(1, n_pen)]
    above = (lax.rem(s + 1, slabs), p)
    below = (lax.rem(s + slabs - 1, slabs), p)
    barrier = pltpu.get_barrier_semaphore()
    greeted = others + peers + members + [above]
    for device in greeted:
        pl.semaphore_signal(barrier, inc=1, device_id=device, device_id_type=MESH)

    for load in loads:
        load.wait()

    u0 = parts(u[0])
    u1 = parts(u[1])
    lx = (left[0, : nx + 16], left[1, : nx + 16])
    select_x = left[0, nx + 16 :]
    pz = (fixed[0], fixed[1])
    select_z = fixed[2]
    t0 = dot3(lx, u0, True)
    tc = dot(select_x, u0[0], True) + dot(select_x, u0[1], True)
    t1 = dot3(lx, u1, True)
    y0 = dot3(parts(t0), pz)
    y1 = dot3(parts(t1), pz)
    tc = parts(tc)
    c = dot(tc[0], select_z) + dot(tc[1], select_z)
    coarse_t[:nx, :] = c

    z_ends = lift[0:1, :], lift[1:2, :]
    d = c[:, 0:1] * z_ends[0] + c[:, nz - 1 : nz] * z_ends[1]
    cz = c - d
    cz_first, cz_last = cz[0:1, :], cz[nx - 1 : nx, :]
    ex = ends[:, 2:3] * cz_first + ends[:, 3:4] * cz_last
    rows8 = lax.broadcasted_iota(jnp.int32, (STATE_ROWS, nz), 0)
    czx_state = jnp.where(
        rows8 == 0,
        pens[p, 2 * n_pen] * cz_first + pens[p, 2 * n_pen + 1] * cz_last,
        pens[p, 2 * n_pen + 2] * cz_first + pens[p, 2 * n_pen + 3] * cz_last,
    )
    czx = cz + ex
    s0 = jnp.where(s == 0, F32(0.5), F32(0.0))
    s1 = jnp.where(s == 0, F32(-1.0 / 12.0), jnp.where(s == slabs - 1, F32(-0.8), F32(0.0)))
    p0 = y0[:nx] + s0 * czx
    p1 = y1[:nx] + s1 * czx
    n0 = y0[nx : nx + STATE_ROWS] + s0 * czx_state
    n1 = y1[nx + STATE_ROWS : nx + 2 * STATE_ROWS] + s1 * jnp.roll(czx_state, 2, 0)
    out_a[:, 0:part, :] = p0.reshape(GROUP, part, nz)
    out_a[:, part : 2 * part, :] = p1.reshape(GROUP, part, nz)
    out_a[:, 2 * part :, :] = jnp.broadcast_to(
        jnp.where(rows8 < 2, n0, n1)[None], (GROUP, STATE_ROWS, nz)
    )
    in_a[m] = out_a[m]
    halo_out[...] = c[0:8, :]

    pl.semaphore_wait(barrier, len(greeted))

    copies_a = []
    for k in range(1, GROUP):
        to = lax.rem(m + k, GROUP)
        copy = pltpu.make_async_remote_copy(
            src_ref=out_a.at[to], dst_ref=in_a.at[m], send_sem=a_send.at[k], recv_sem=a_recv.at[k],
            device_id=(g * GROUP + to, p), device_id_type=MESH,
        )
        copy.start()
        copies_a.append(copy)
    copy_h1 = pltpu.make_async_remote_copy(
        src_ref=halo_out, dst_ref=halo_in, send_sem=h1_send, recv_sem=h1_recv,
        device_id=(s, lax.rem(p + n_pen - 1, n_pen)), device_id_type=MESH,
    )
    copy_h1.start()

    in_b[g] = jnp.zeros((part + STATE_ROWS, nz), F32)
    rest = d - ex

    copy_h1.wait_recv()
    halo = jnp.where(p == n_pen - 1, c[nx - 1 : nx, :], halo_in[0:1, :])
    coarse_t[nx : nx + 8, :] = jnp.broadcast_to(halo, (8, nz))
    copy_h2 = pltpu.make_async_remote_copy(
        src_ref=coarse_t, dst_ref=next_c, send_sem=h2_send, recv_sem=h2_recv,
        device_id=below, device_id_type=MESH,
    )
    copy_h2.start()

    fine_rows = lax.broadcasted_iota(jnp.int32, (2 * nx, nz), 0)

    def interpolant(values, beyond):
        high, low = parts(values)
        along_x = dot(fixed[3], high) + dot(fixed[3], low)
        along_x = along_x + jnp.where(fine_rows == 2 * nx - 1, 0.5 * beyond, 0.0)
        high, low = parts(along_x)
        return dot(fixed[4], high, True) + dot(fixed[4], low, True)

    zi = lax.broadcasted_iota(jnp.int32, (2 * nz, 2 * nx), 0)
    xi = lax.broadcasted_iota(jnp.int32, (2 * nz, 2 * nx), 1)
    kept = ((zi | xi) & 1) == 0
    fine[0] = jnp.where(kept, 0.0, u[0] - interpolant(c, halo))

    for copy in copies_a:
        copy.wait_recv()

    def weigh(base, step, count, get):
        total = table[g, base] * get(0)
        for k in range(1, count):
            total = total + table[g, base + k * step] * get(k)
        return total

    def plane(k):
        return in_a[k // 2, (k % 2) * part : (k % 2 + 1) * part, :]

    def state(k):
        return in_a[k, 2 * part :, :]

    def states(base):
        even = weigh(base, 2, GROUP, state)
        odd = weigh(base + 1, 2, GROUP, state)
        return even + jnp.roll(odd, STATE_ROWS - 2, 0)

    for way, base in ((0, at.to_later), (1, at.to_earlier)):
        out_b[way, :part, :] = weigh(base, 1, 2 * GROUP, plane)
        out_b[way, part:, :] = states(base)
    copies_b = []
    for k in range(1, groups):
        to = lax.rem(g + k, groups)
        copy = pltpu.make_async_remote_copy(
            src_ref=out_b.at[jnp.where(to > g, 0, 1)], dst_ref=in_b.at[g],
            send_sem=b_send.at[k], recv_sem=b_recv.at[k],
            device_id=(to * GROUP + m, p), device_id_type=MESH,
        )
        copy.start()
        copies_b.append(copy)

    for i in range(GROUP):
        out_c[i] = weigh(at.local + 2 * GROUP * i, 1, 2 * GROUP, plane)
    own_states = states(at.local + 2 * GROUP * m)

    copy_h2.wait_recv()
    last = s == slabs - 1
    after = jnp.where(last, coarse_t[...], next_c[...])
    middle = 0.5 * (coarse_t[...] + after)
    fine[1] = u[1] - interpolant(middle[:nx], middle[nx : nx + 1])
    store_odd = pltpu.make_async_copy(fine.at[1], fine_hbm.at[1], store_sem.at[0])
    store_odd.start()

    for copy in copies_b:
        copy.wait_recv()
    from_earlier = weigh(at.from_earlier, 1, groups, lambda k: in_b[k])
    from_later = weigh(at.from_later, 1, groups, lambda k: in_b[k])
    own_states = (
        own_states
        + table[g, at.falling + m] * from_earlier[part:]
        + table[g, at.rising + m] * from_later[part:]
        - czx_state
    )
    out_x[...] = own_states
    copies_x = []
    for k in range(1, n_pen):
        copy = pltpu.make_async_remote_copy(
            src_ref=out_x, dst_ref=in_x.at[p], send_sem=x_send.at[k], recv_sem=x_recv.at[k],
            device_id=(s, lax.rem(p + k, n_pen)), device_id_type=MESH,
        )
        copy.start()
        copies_x.append(copy)
    for i in range(GROUP):
        out_c[i] = (
            out_c[i]
            + table[g, at.falling + i] * from_earlier[:part]
            + table[g, at.rising + i] * from_later[:part]
        )
    copies_c = []
    for k in range(1, GROUP):
        to = lax.rem(m + k, GROUP)
        copy = pltpu.make_async_remote_copy(
            src_ref=out_c.at[to], dst_ref=in_c.at[m], send_sem=c_send.at[k], recv_sem=c_recv.at[k],
            device_id=(g * GROUP + to, p), device_id_type=MESH,
        )
        copy.start()
        copies_c.append(copy)
    in_c[m] = out_c[m]
    in_x[p] = out_x[...]

    for copy in copies_x:
        copy.wait_recv()
    x_earlier = pens[p, 0] * in_x[0, 0:1, :]
    x_later = pens[p, n_pen] * in_x[0, 1:2, :]
    for k in range(1, n_pen):
        x_earlier = x_earlier + pens[p, k] * in_x[k, 0:1, :]
        x_later = x_later + pens[p, n_pen + k] * in_x[k, 1:2, :]
    rest = rest + ends[:, 0:1] * x_earlier + ends[:, 1:2] * x_later
    for copy in copies_c:
        copy.wait_recv()
    values = (in_c[...].reshape(nx, nz) + rest).T
    coarse[...] = values
    store_coarse = pltpu.make_async_copy(coarse, coarse_hbm.at[0], store_sem.at[1])
    store_coarse.start()
    high, low = parts(values)
    spread = dot(select_z, high) + dot(select_z, low)
    high, low = parts(spread)
    fine[0] = fine[0] + dot(high, select_x) + dot(low, select_x)
    store_even = pltpu.make_async_copy(fine.at[0], fine_hbm.at[0], store_sem.at[2])
    store_even.start()

    for copy in copies_a + copies_b + copies_c + copies_x + [copy_h1, copy_h2]:
        copy.wait_send()
    store_odd.wait()
    store_coarse.wait()
    store_even.wait()


def tables(slabs, n_pen, nx, nz):
    groups = slabs // GROUP
    bx = Blocks(nx * n_pen, n_pen)
    by = Blocks(slabs, groups)
    bz = Blocks(nz, 1)

    pz_high, pz_low = split(bz.diagonal[0].T)
    select = np.zeros((2 * nz, nz))
    select[2 * np.arange(nz), np.arange(nz)] = 1.0
    inner = refine_matrix(nx)
    inner[2 * nx - 1, nx - 1] = 0.5
    fixed = np.stack(
        [pz_high, pz_low, split(select)[0], split(inner)[0], split(refine_matrix(nz))[0]]
    )

    left = np.zeros((n_pen, 2, 2 * nx + 16, 2 * nx), ml_dtypes.bfloat16)
    ends = np.zeros((n_pen, nx, 128), np.float32)
    pens = np.zeros((n_pen, 2 * n_pen + 4), np.float32)
    for b in range(n_pen):
        states = np.zeros((16, 2 * nx))
        states[0] = states[10] = bx.to_later[b]
        states[1] = states[11] = bx.to_earlier[b]
        block = split(np.concatenate([bx.diagonal[b], states]))
        left[b, 0, : nx + 16], left[b, 1, : nx + 16] = block
        left[b, 0, nx + 16 + np.arange(nx), 2 * np.arange(nx)] = 1.0
        ends[b, :, 0] = bx.falling[b]
        ends[b, :, 1] = bx.rising[b]
        pens[b, :n_pen] = bx.from_earlier[b]
        pens[b, n_pen : 2 * n_pen] = bx.from_later[b]
        if b == 0:
            ends[b, :, 2] = -bx.own_first / 3.0
            pens[b, 2 * n_pen] = -bx.first_to_later / 3.0
        if b == n_pen - 1:
            ends[b, :, 3] = bx.own_last * 2.0 / 3.0
            pens[b, 2 * n_pen + 3] = bx.last_to_earlier * 2.0 / 3.0

    at = Scalars(groups)
    table = np.zeros((groups, at.size), np.float32)
    for b in range(groups):
        table[b, at.local : at.to_later] = by.diagonal[b].reshape(-1)
        table[b, at.to_later : at.to_earlier] = by.to_later[b]
        table[b, at.to_earlier : at.falling] = by.to_earlier[b]
        table[b, at.falling : at.rising] = by.falling[b]
        table[b, at.rising : at.from_earlier] = by.rising[b]
        table[b, at.from_earlier : at.from_later] = by.from_earlier[b]
        table[b, at.from_later :] = by.from_later[b]

    inverse = inverse_mass(nz)
    lift = np.zeros((8, nz), np.float32)
    lift[0] = inverse[:, 0] / 3.0
    lift[1] = inverse[:, -1] * (-2.0 / 3.0)
    return at, fixed, left, ends, table, pens, lift


def per_device(slabs, n_pen, density):
    nz, nx = density.shape[1] // 2, density.shape[2] // 2
    groups = slabs // GROUP
    part = nx // GROUP
    at, fixed, left, ends, table, pens, lift = tables(slabs, n_pen, nx, nz)
    anywhere = pl.BlockSpec(memory_space=pl.ANY)
    scalars = pl.BlockSpec(memory_space=pltpu.SMEM)
    vector = pl.BlockSpec(memory_space=pltpu.VMEM)
    dma = pltpu.SemaphoreType.DMA

    def body(u_hbm, fixed_hbm, left_hbm, ends_hbm, table, pens, lift, fine_hbm, coarse_hbm, *rest):
        (u, fixed, left, ends, coarse_t, halo_in, halo_out, next_c, *more) = rest
        kernel(
            (slabs, n_pen, groups, nx, nz, at),
            u_hbm, fixed_hbm, left_hbm, ends_hbm, table, pens, fine_hbm, coarse_hbm,
            u, fixed, left, ends, coarse_t, halo_in, halo_out, next_c, lift, *more,
        )

    return pl.pallas_call(
        body,
        out_shape=(
            jax.ShapeDtypeStruct(density.shape, F32),
            jax.ShapeDtypeStruct((1, nz, nx), F32),
        ),
        in_specs=[anywhere, anywhere, anywhere, anywhere, scalars, scalars, vector],
        out_specs=(anywhere, anywhere),
        scratch_shapes=[
            pltpu.VMEM(density.shape, F32),
            pltpu.VMEM(fixed.shape, BF16),
            pltpu.VMEM(left.shape[1:], BF16),
            pltpu.VMEM(ends.shape[1:], F32),
            pltpu.VMEM((nx + 8, nz), F32),
            pltpu.VMEM((8, nz), F32),
            pltpu.VMEM((8, nz), F32),
            pltpu.VMEM((nx + 8, nz), F32),
            pltpu.VMEM((GROUP, 2 * part + STATE_ROWS, nz), F32),
            pltpu.VMEM((GROUP, 2 * part + STATE_ROWS, nz), F32),
            pltpu.VMEM((2, part + STATE_ROWS, nz), F32),
            pltpu.VMEM((groups, part + STATE_ROWS, nz), F32),
            pltpu.VMEM((GROUP, part, nz), F32),
            pltpu.VMEM((GROUP, part, nz), F32),
            pltpu.VMEM((STATE_ROWS, nz), F32),
            pltpu.VMEM((n_pen, STATE_ROWS, nz), F32),
            pltpu.VMEM(density.shape, F32),
            pltpu.VMEM((nz, nx), F32),
            dma((4,)),
            dma((3,)),
            dma, dma, dma, dma,
            dma((GROUP,)), dma((GROUP,)), dma((groups,)), dma((groups,)),
            dma((GROUP,)), dma((GROUP,)), dma((n_pen,)), dma((n_pen,)),
        ],
        compiler_params=pltpu.CompilerParams(
            collective_id=0, has_side_effects=True, vmem_limit_bytes=32 * 1024 * 1024
        ),
        name="decompose",
    )(density, fixed, left, ends, table, pens, lift)


def solution(mesh):
    slabs, n_pen = mesh.shape["slab"], mesh.shape["pen"]
    return jax.shard_map(
        functools.partial(per_device, slabs, n_pen),
        mesh=mesh,
        in_specs=(P("slab", None, "pen"),),
        out_specs=(P("slab", None, "pen"), P("slab", None, "pen")),
        check_vma=False,
    )
```

profile of v0, /device:TPU:1, one launch (start us, length us, event | category | flops | bytes accessed | tf_op | source)
XLA Modules:
  0.0 46.0 jit_solution(16878818999731511372)
XLA Ops:
  0.6 0.0 copy-start
  0.6 1.6 %copy-done = bf16[8,2,272,256]{3,2,1,0:T(8,128)(2,1)S(1)} copy-done((bf16[8,2,272,256]{3,2,1,0:T(8,128)(2,1)S(1)}, bf16[8,2,272,256]{3,2,1,0:T(8,128)(2,1)}, u32[]{:S(2)}) %copy-start) | copy-done | bytes 2228248
  2.3 0.0 copy-start.1
  2.3 1.0 %copy-done.1 = f32[2,256,256]{2,1,0:T(8,128)S(1)} copy-done((f32[2,256,256]{2,1,0:T(8,128)S(1)}, f32[2,256,256]{2,1,0:T(8,128)}, u32[]{:S(2)}) %copy-start.1) | copy-done | bytes 524312
  3.3 0.0 copy-start.2
  3.3 1.0 %copy-done.2 = f32[8,128,128]{2,1,0:T(8,128)S(1)} copy-done((f32[8,128,128]{2,1,0:T(8,128)S(1)}, f32[8,128,128]{2,1,0:T(8,128)}, u32[]{:S(2)}) %copy-start.2) | copy-done | bytes 524312
  4.3 0.0 copy-start.3
  4.3 1.0 %copy-done.3 = bf16[5,256,128]{2,1,0:T(8,128)(2,1)S(1)} copy-done((bf16[5,256,128]{2,1,0:T(8,128)(2,1)S(1)}, bf16[5,256,128]{2,1,0:T(8,128)(2,1)}, u32[]{:S(2)}) %copy-start.3) | copy-done | bytes 327704
  5.3 0.0 copy-start.4
  5.3 0.7 %copy-done.4 = f32[8,192]{1,0:T(8,128)S(1)} copy-done((f32[8,192]{1,0:T(8,128)S(1)}, f32[8,192]{1,0:T(8,128)}, u32[]{:S(2)}) %copy-start.4) | copy-done | bytes 6168
  6.0 0.0 copy-start.5
  6.0 0.7 %copy-done.5 = f32[8,128]{1,0:T(8,128)S(1)} copy-done((f32[8,128]{1,0:T(8,128)S(1)}, f32[8,128]{1,0:T(8,128)}, u32[]{:S(2)}) %copy-start.5) | copy-done | bytes 4120
  6.7 0.0 copy-start.6
  6.7 0.7 %copy-done.6 = f32[8,20]{1,0:T(8,128)S(1)} copy-done((f32[8,20]{1,0:T(8,128)S(1)}, f32[8,20]{1,0:T(8,128)}, u32[]{:S(2)}) %copy-start.6) | copy-done | bytes 664
  7.4 37.1 %decompose.1 = (f32[2,256,256]{2,1,0:T(8,128)S(1)}, f32[1,128,128]{2,1,0:T(8,128)S(1)}) custom-call(f32[2,256,256]{2,1,0:T(8,128)S(1)} %copy-done.1, bf16[5,256,128]{2,1,0:T(8,128)(2,1)S(1)} %copy-done.3, bf16[8,2,272,256]{3,2,1,0:T(8,128)(2,1)S(1)} %copy-done, f32[8,128,128]{2,1,0:T(8,128)S(1)} %copy-done.2, f32[8,192]{1,0:T(8,128)S(1)} %copy-done.4, ...), custom_call_target="tpu_custom_call" | custom-call | tf_op jit(solution)/shard_map/decompose/pallas_call | solution.py:448
  44.5 0.8 %copy.11 = f32[2,256,256]{2,1,0:T(8,128)} copy(f32[2,256,256]{2,1,0:T(8,128)S(1)} %get-tuple-element.4) | data formatting | bytes 1048576
  45.3 0.6 %copy.12 = f32[1,128,128]{2,1,0:T(8,128)} copy(f32[1,128,128]{2,1,0:T(8,128)S(1)} %get-tuple-element.5) | data formatting | bytes 131072
Async XLA Ops:
  0.6 1.6 %copy-start = (bf16[8,2,272,256]{3,2,1,0:T(8,128)(2,1)S(1)}, bf16[8,2,272,256]{3,2,1,0:T(8,128)(2,1)}, u32[]{:S(2)}) copy-start(bf16[8,2,272,256]{3,2,1,0:T(8,128)(2,1)} %constant.13.clone.left_hbm) | copy-start | bytes 6684676
  2.3 1.0 %copy-start.1 = (f32[2,256,256]{2,1,0:T(8,128)S(1)}, f32[2,256,256]{2,1,0:T(8,128)}, u32[]{:S(2)}) copy-start(f32[2,256,256]{2,1,0:T(8,128)} %u_hbm.1) | copy-start | bytes 1572868
  3.3 1.0 %copy-start.2 = (f32[8,128,128]{2,1,0:T(8,128)S(1)}, f32[8,128,128]{2,1,0:T(8,128)}, u32[]{:S(2)}) copy-start(f32[8,128,128]{2,1,0:T(8,128)} %constant.14.clone.ends_hbm) | copy-start | bytes 1572868
  4.3 1.0 %copy-start.3 = (bf16[5,256,128]{2,1,0:T(8,128)(2,1)S(1)}, bf16[5,256,128]{2,1,0:T(8,128)(2,1)}, u32[]{:S(2)}) copy-start(bf16[5,256,128]{2,1,0:T(8,128)(2,1)} %constant.12.clone.fixed_hbm) | copy-start | bytes 983044
  5.3 0.7 %copy-start.4 = (f32[8,192]{1,0:T(8,128)S(1)}, f32[8,192]{1,0:T(8,128)}, u32[]{:S(2)}) copy-start(f32[8,192]{1,0:T(8,128)} %constant.15.clone.table) | copy-start | bytes 18436
  6.0 0.7 %copy-start.5 = (f32[8,128]{1,0:T(8,128)S(1)}, f32[8,128]{1,0:T(8,128)}, u32[]{:S(2)}) copy-start(f32[8,128]{1,0:T(8,128)} %constant.17.clone.lift) | copy-start | bytes 12292
  6.7 0.7 %copy-start.6 = (f32[8,20]{1,0:T(8,128)S(1)}, f32[8,20]{1,0:T(8,128)}, u32[]{:S(2)}) copy-start(f32[8,20]{1,0:T(8,128)} %constant.16.clone.pens) | copy-start | bytes 1924
where the time goes:
time: 46.3 us; the launch traced here: 46 us
  Pallas kernels  37.1 us (80%)
  local copies, waits for them, and re-layouts  8.17 us (18%)
  between operations  0.65 us (1%)
    pallas_call x1, Pallas kernels, per_device(): pl.pallas_call(body, out_shape=(jax.ShapeDtypeStruct(density.shape, F32),...  37.1 us
    unnamed x16, local copies, waits for them, and re-layouts  8.17 us

commit v1 on v0

--- a/solution.py
+++ b/solution.py
@@ -140,14 +140,14 @@
 
 def kernel(
     sizes,
-    u_hbm, fixed_hbm, left_hbm, ends_hbm, table, pens,
+    u_hbm, fixed_hbm, left_hbm, ends_hbm, table_hbm,
     fine_hbm, coarse_hbm,
-    u, fixed, left, ends, coarse_t, halo_in, halo_out, next_c, lift,
+    u, fixed, left, ends, table, coarse_t, halo_in, halo_out, next_c,
     out_a, in_a, out_b, in_b, out_c, in_c, out_x, in_x,
     fine, coarse,
     load_sem, store_sem,
     h1_send, h1_recv, h2_send, h2_recv,
-    a_send, a_recv, b_send, b_recv, c_send, c_recv, x_send, x_recv,
+    onward, a_send, a_recv, b_send, b_recv, c_send, c_recv, x_send, x_recv,
 ):
     slabs, n_pen, groups, nx, nz, at = sizes
     part = nx // GROUP
@@ -161,12 +161,22 @@
         pltpu.make_async_copy(fixed_hbm, fixed, load_sem.at[1]),
         pltpu.make_async_copy(left_hbm.at[p], left, load_sem.at[2]),
         pltpu.make_async_copy(ends_hbm.at[p], ends, load_sem.at[3]),
+        pltpu.make_async_copy(table_hbm, table, load_sem.at[4]),
     ]
     for load in loads:
         load.start()
 
+    turns = groups // 2
+    turn, side = lax.rem(g, turns), g // turns
+
+    def group_at(ahead, flips):
+        return lax.rem(side + flips, 2) * turns + lax.rem(turn + ahead, turns)
+
+    steps = sorted(range(turns), key=lambda k: -min(k, turns - k))
+    far_first = [(k, flips) for k in steps for flips in (1, 0) if (k, flips) != (0, 0)]
+    near = [(k, flips) for k, flips in far_first if min(k, turns - k) <= 1]
     members = [(g * GROUP + lax.rem(m + k, GROUP), p) for k in range(1, GROUP)]
-    others = [(lax.rem(g + k, groups) * GROUP + m, p) for k in range(1, groups)]
+    others = [(group_at(*step) * GROUP + m, p) for step in near]
     peers = [(s, lax.rem(p + k, n_pen)) for k in range(1, n_pen)]
     above = (lax.rem(s + 1, slabs), p)
     below = (lax.rem(s + slabs - 1, slabs), p)
@@ -193,16 +203,19 @@
     c = dot(tc[0], select_z) + dot(tc[1], select_z)
     coarse_t[:nx, :] = c
 
-    z_ends = lift[0:1, :], lift[1:2, :]
+    def pen(k):
+        return table[groups + p, k]
+
+    z_ends = ends[nx : nx + 1, :], ends[nx + 1 : nx + 2, :]
     d = c[:, 0:1] * z_ends[0] + c[:, nz - 1 : nz] * z_ends[1]
     cz = c - d
     cz_first, cz_last = cz[0:1, :], cz[nx - 1 : nx, :]
-    ex = ends[:, 2:3] * cz_first + ends[:, 3:4] * cz_last
+    ex = ends[:nx, 2:3] * cz_first + ends[:nx, 3:4] * cz_last
     rows8 = lax.broadcasted_iota(jnp.int32, (STATE_ROWS, nz), 0)
     czx_state = jnp.where(
         rows8 == 0,
-        pens[p, 2 * n_pen] * cz_first + pens[p, 2 * n_pen + 1] * cz_last,
-        pens[p, 2 * n_pen + 2] * cz_first + pens[p, 2 * n_pen + 3] * cz_last,
+        pen(2 * n_pen) * cz_first + pen(2 * n_pen + 1) * cz_last,
+        pen(2 * n_pen + 2) * cz_first + pen(2 * n_pen + 3) * cz_last,
     )
     czx = cz + ex
     s0 = jnp.where(s == 0, F32(0.5), F32(0.0))
@@ -230,6 +243,8 @@
         )
         copy.start()
         copies_a.append(copy)
+    behind = (group_at(turns - 1, 0) * GROUP + m, p)
+    pl.semaphore_signal(onward, inc=1, device_id=behind, device_id_type=MESH)
     copy_h1 = pltpu.make_async_remote_copy(
         src_ref=halo_out, dst_ref=halo_in, send_sem=h1_send, recv_sem=h1_recv,
         device_id=(s, lax.rem(p + n_pen - 1, n_pen)), device_id_type=MESH,
@@ -285,9 +300,10 @@
     for way, base in ((0, at.to_later), (1, at.to_earlier)):
         out_b[way, :part, :] = weigh(base, 1, 2 * GROUP, plane)
         out_b[way, part:, :] = states(base)
+    pl.semaphore_wait(onward, 1)
     copies_b = []
-    for k in range(1, groups):
-        to = lax.rem(g + k, groups)
+    for k, step in enumerate(far_first):
+        to = group_at(*step)
         copy = pltpu.make_async_remote_copy(
             src_ref=out_b.at[jnp.where(to > g, 0, 1)], dst_ref=in_b.at[g],
             send_sem=b_send.at[k], recv_sem=b_recv.at[k],
@@ -347,12 +363,12 @@
 
     for copy in copies_x:
         copy.wait_recv()
-    x_earlier = pens[p, 0] * in_x[0, 0:1, :]
-    x_later = pens[p, n_pen] * in_x[0, 1:2, :]
+    x_earlier = pen(0) * in_x[0, 0:1, :]
+    x_later = pen(n_pen) * in_x[0, 1:2, :]
     for k in range(1, n_pen):
-        x_earlier = x_earlier + pens[p, k] * in_x[k, 0:1, :]
-        x_later = x_later + pens[p, n_pen + k] * in_x[k, 1:2, :]
-    rest = rest + ends[:, 0:1] * x_earlier + ends[:, 1:2] * x_later
+        x_earlier = x_earlier + pen(k) * in_x[k, 0:1, :]
+        x_later = x_later + pen(n_pen + k) * in_x[k, 1:2, :]
+    rest = rest + ends[:nx, 0:1] * x_earlier + ends[:nx, 1:2] * x_later
     for copy in copies_c:
         copy.wait_recv()
     values = (in_c[...].reshape(nx, nz) + rest).T
@@ -389,7 +405,10 @@
     )
 
     left = np.zeros((n_pen, 2, 2 * nx + 16, 2 * nx), ml_dtypes.bfloat16)
-    ends = np.zeros((n_pen, nx, 128), np.float32)
+    inverse = inverse_mass(nz)
+    ends = np.zeros((n_pen, nx + 8, nz), np.float32)
+    ends[:, nx] = inverse[:, 0] / 3.0
+    ends[:, nx + 1] = inverse[:, -1] * (-2.0 / 3.0)
     pens = np.zeros((n_pen, 2 * n_pen + 4), np.float32)
     for b in range(n_pen):
         states = np.zeros((16, 2 * nx))
@@ -398,19 +417,20 @@
         block = split(np.concatenate([bx.diagonal[b], states]))
         left[b, 0, : nx + 16], left[b, 1, : nx + 16] = block
         left[b, 0, nx + 16 + np.arange(nx), 2 * np.arange(nx)] = 1.0
-        ends[b, :, 0] = bx.falling[b]
-        ends[b, :, 1] = bx.rising[b]
+        ends[b, :nx, 0] = bx.falling[b]
+        ends[b, :nx, 1] = bx.rising[b]
         pens[b, :n_pen] = bx.from_earlier[b]
         pens[b, n_pen : 2 * n_pen] = bx.from_later[b]
         if b == 0:
-            ends[b, :, 2] = -bx.own_first / 3.0
+            ends[b, :nx, 2] = -bx.own_first / 3.0
             pens[b, 2 * n_pen] = -bx.first_to_later / 3.0
         if b == n_pen - 1:
-            ends[b, :, 3] = bx.own_last * 2.0 / 3.0
+            ends[b, :nx, 3] = bx.own_last * 2.0 / 3.0
             pens[b, 2 * n_pen + 3] = bx.last_to_earlier * 2.0 / 3.0
 
     at = Scalars(groups)
-    table = np.zeros((groups, at.size), np.float32)
+    table = np.zeros((groups + n_pen, at.size), np.float32)
+    table[groups:, : pens.shape[1]] = pens
     for b in range(groups):
         table[b, at.local : at.to_later] = by.diagonal[b].reshape(-1)
         table[b, at.to_later : at.to_earlier] = by.to_later[b]
@@ -419,45 +439,30 @@
         table[b, at.rising : at.from_earlier] = by.rising[b]
         table[b, at.from_earlier : at.from_later] = by.from_earlier[b]
         table[b, at.from_later :] = by.from_later[b]
-
-    inverse = inverse_mass(nz)
-    lift = np.zeros((8, nz), np.float32)
-    lift[0] = inverse[:, 0] / 3.0
-    lift[1] = inverse[:, -1] * (-2.0 / 3.0)
-    return at, fixed, left, ends, table, pens, lift
+    return at, fixed, left, ends, table
 
 
 def per_device(slabs, n_pen, density):
     nz, nx = density.shape[1] // 2, density.shape[2] // 2
     groups = slabs // GROUP
     part = nx // GROUP
-    at, fixed, left, ends, table, pens, lift = tables(slabs, n_pen, nx, nz)
+    at, fixed, left, ends, table = tables(slabs, n_pen, nx, nz)
     anywhere = pl.BlockSpec(memory_space=pl.ANY)
-    scalars = pl.BlockSpec(memory_space=pltpu.SMEM)
-    vector = pl.BlockSpec(memory_space=pltpu.VMEM)
     dma = pltpu.SemaphoreType.DMA
-
-    def body(u_hbm, fixed_hbm, left_hbm, ends_hbm, table, pens, lift, fine_hbm, coarse_hbm, *rest):
-        (u, fixed, left, ends, coarse_t, halo_in, halo_out, next_c, *more) = rest
-        kernel(
-            (slabs, n_pen, groups, nx, nz, at),
-            u_hbm, fixed_hbm, left_hbm, ends_hbm, table, pens, fine_hbm, coarse_hbm,
-            u, fixed, left, ends, coarse_t, halo_in, halo_out, next_c, lift, *more,
-        )
-
     return pl.pallas_call(
-        body,
+        functools.partial(kernel, (slabs, n_pen, groups, nx, nz, at)),
         out_shape=(
             jax.ShapeDtypeStruct(density.shape, F32),
             jax.ShapeDtypeStruct((1, nz, nx), F32),
         ),
-        in_specs=[anywhere, anywhere, anywhere, anywhere, scalars, scalars, vector],
+        in_specs=[pl.BlockSpec(memory_space=pltpu.HBM)] * 5,
         out_specs=(anywhere, anywhere),
         scratch_shapes=[
             pltpu.VMEM(density.shape, F32),
             pltpu.VMEM(fixed.shape, BF16),
             pltpu.VMEM(left.shape[1:], BF16),
             pltpu.VMEM(ends.shape[1:], F32),
+            pltpu.SMEM(table.shape, F32),
             pltpu.VMEM((nx + 8, nz), F32),
             pltpu.VMEM((8, nz), F32),
             pltpu.VMEM((8, nz), F32),
@@ -472,9 +477,10 @@
             pltpu.VMEM((n_pen, STATE_ROWS, nz), F32),
             pltpu.VMEM(density.shape, F32),
             pltpu.VMEM((nz, nx), F32),
-            dma((4,)),
+            dma((5,)),
             dma((3,)),
             dma, dma, dma, dma,
+            pltpu.SemaphoreType.REGULAR,
             dma((GROUP,)), dma((GROUP,)), dma((groups,)), dma((groups,)),
             dma((GROUP,)), dma((GROUP,)), dma((n_pen,)), dma((n_pen,)),
         ],
@@ -482,7 +488,7 @@
             collective_id=0, has_side_effects=True, vmem_limit_bytes=32 * 1024 * 1024
         ),
         name="decompose",
-    )(density, fixed, left, ends, table, pens, lift)
+    )(density, fixed, left, ends, table)
 
 
 def solution(mesh):

time: 46.3 us -> 44.1 us (0.952)
  local copies, waits for them, and re-layouts: 8.17 us -> 6.83 us
  Pallas kernels: 37.1 us -> 36.3 us
    unnamed x16 -> x12, local copies, waits for them, and re-layouts: 8.17 us -> 6.83 us
    pallas_call x1, Pallas kernels: 37.1 us -> 36.3 us  [per_device(): pl.pallas_call(functools.partial(kernel, (slabs, n_pen, groups, nx, nz, a...]
where the time goes in v1:
time: 44.1 us; the launch traced here: 43.8 us
  Pallas kernels  36.3 us (82%)
  local copies, waits for them, and re-layouts  6.83 us (15%)
  between operations  0.65 us (1%)
    pallas_call x1, Pallas kernels, per_device(): pl.pallas_call(functools.partial(kernel, (slabs, n_pen, groups, nx, nz, a...  36.3 us
    unnamed x12, local copies, waits for them, and re-layouts  6.83 us

profile of v1, /device:TPU:1, one launch (start us, length us, event | category | flops | bytes accessed | tf_op | source)
XLA Modules:
  0.0 43.8 jit_solution(616726304494531769)
XLA Ops:
  0.6 0.0 copy-start
  0.6 1.6 %copy-done = bf16[8,2,272,256]{3,2,1,0:T(8,128)(2,1)S(1)} copy-done((bf16[8,2,272,256]{3,2,1,0:T(8,128)(2,1)S(1)}, bf16[8,2,272,256]{3,2,1,0:T(8,128)(2,1)}, u32[]{:S(2)}) %copy-start) | copy-done | bytes 2228248
  2.3 0.0 copy-start.1
  2.3 1.1 %copy-done.1 = f32[8,136,128]{2,1,0:T(8,128)S(1)} copy-done((f32[8,136,128]{2,1,0:T(8,128)S(1)}, f32[8,136,128]{2,1,0:T(8,128)}, u32[]{:S(2)}) %copy-start.1) | copy-done | bytes 557080
  3.3 0.0 copy-start.2
  3.3 1.0 %copy-done.2 = f32[2,256,256]{2,1,0:T(8,128)S(1)} copy-done((f32[2,256,256]{2,1,0:T(8,128)S(1)}, f32[2,256,256]{2,1,0:T(8,128)}, u32[]{:S(2)}) %copy-start.2) | copy-done | bytes 524312
  4.4 0.0 copy-start.3
  4.4 1.0 %copy-done.3 = bf16[5,256,128]{2,1,0:T(8,128)(2,1)S(1)} copy-done((bf16[5,256,128]{2,1,0:T(8,128)(2,1)S(1)}, bf16[5,256,128]{2,1,0:T(8,128)(2,1)}, u32[]{:S(2)}) %copy-start.3) | copy-done | bytes 327704
  5.3 0.0 copy-start.4
  5.3 0.7 %copy-done.4 = f32[16,192]{1,0:T(8,128)S(1)} copy-done((f32[16,192]{1,0:T(8,128)S(1)}, f32[16,192]{1,0:T(8,128)}, u32[]{:S(2)}) %copy-start.4) | copy-done | bytes 12312
  6.0 36.3 %decompose.1 = (f32[2,256,256]{2,1,0:T(8,128)S(1)}, f32[1,128,128]{2,1,0:T(8,128)S(1)}) custom-call(f32[2,256,256]{2,1,0:T(8,128)S(1)} %copy-done.2, bf16[5,256,128]{2,1,0:T(8,128)(2,1)S(1)} %copy-done.3, bf16[8,2,272,256]{3,2,1,0:T(8,128)(2,1)S(1)} %copy-done, f32[8,136,128]{2,1,0:T(8,128)S(1)} %copy-done.1, f32[16,192]{1,0:T(8,128)S(1)} %copy-done.4), custom_call_target="tpu_custom_call" | custom-call | tf_op jit(solution)/shard_map/decompose/pallas_call | solution.py:452
  42.4 0.8 %copy.9 = f32[2,256,256]{2,1,0:T(8,128)} copy(f32[2,256,256]{2,1,0:T(8,128)S(1)} %get-tuple-element.4) | data formatting | bytes 1048576
  43.2 0.6 %copy.10 = f32[1,128,128]{2,1,0:T(8,128)} copy(f32[1,128,128]{2,1,0:T(8,128)S(1)} %get-tuple-element.5) | data formatting | bytes 131072
Async XLA Ops:
  0.6 1.6 %copy-start = (bf16[8,2,272,256]{3,2,1,0:T(8,128)(2,1)S(1)}, bf16[8,2,272,256]{3,2,1,0:T(8,128)(2,1)}, u32[]{:S(2)}) copy-start(bf16[8,2,272,256]{3,2,1,0:T(8,128)(2,1)} %constant.9.clone.left_hbm) | copy-start | bytes 6684676
  2.3 1.1 %copy-start.1 = (f32[8,136,128]{2,1,0:T(8,128)S(1)}, f32[8,136,128]{2,1,0:T(8,128)}, u32[]{:S(2)}) copy-start(f32[8,136,128]{2,1,0:T(8,128)} %constant.10.clone.ends_hbm) | copy-start | bytes 1671172
  3.3 1.0 %copy-start.2 = (f32[2,256,256]{2,1,0:T(8,128)S(1)}, f32[2,256,256]{2,1,0:T(8,128)}, u32[]{:S(2)}) copy-start(f32[2,256,256]{2,1,0:T(8,128)} %u_hbm.1) | copy-start | bytes 1572868
  4.4 1.0 %copy-start.3 = (bf16[5,256,128]{2,1,0:T(8,128)(2,1)S(1)}, bf16[5,256,128]{2,1,0:T(8,128)(2,1)}, u32[]{:S(2)}) copy-start(bf16[5,256,128]{2,1,0:T(8,128)(2,1)} %constant.8.clone.fixed_hbm) | copy-start | bytes 983044
  5.3 0.7 %copy-start.4 = (f32[16,192]{1,0:T(8,128)S(1)}, f32[16,192]{1,0:T(8,128)}, u32[]{:S(2)}) copy-start(f32[16,192]{1,0:T(8,128)} %constant.11.clone.table_hbm) | copy-start | bytes 36868

commit v2 on v1

--- a/solution.py
+++ b/solution.py
@@ -141,11 +141,10 @@
 def kernel(
     sizes,
     u_hbm, fixed_hbm, left_hbm, ends_hbm, table_hbm,
-    fine_hbm, coarse_hbm,
+    fine, coarse,
     u, fixed, left, ends, table, coarse_t, halo_in, halo_out, next_c,
     out_a, in_a, out_b, in_b, out_c, in_c, out_x, in_x,
-    fine, coarse,
-    load_sem, store_sem,
+    load_sem,
     h1_send, h1_recv, h2_send, h2_recv,
     onward, a_send, a_recv, b_send, b_recv, c_send, c_recv, x_send, x_recv,
 ):
@@ -321,8 +320,6 @@
     after = jnp.where(last, coarse_t[...], next_c[...])
     middle = 0.5 * (coarse_t[...] + after)
     fine[1] = u[1] - interpolant(middle[:nx], middle[nx : nx + 1])
-    store_odd = pltpu.make_async_copy(fine.at[1], fine_hbm.at[1], store_sem.at[0])
-    store_odd.start()
 
     for copy in copies_b:
         copy.wait_recv()
@@ -372,21 +369,14 @@
     for copy in copies_c:
         copy.wait_recv()
     values = (in_c[...].reshape(nx, nz) + rest).T
-    coarse[...] = values
-    store_coarse = pltpu.make_async_copy(coarse, coarse_hbm.at[0], store_sem.at[1])
-    store_coarse.start()
+    coarse[0] = values
     high, low = parts(values)
     spread = dot(select_z, high) + dot(select_z, low)
     high, low = parts(spread)
     fine[0] = fine[0] + dot(high, select_x) + dot(low, select_x)
-    store_even = pltpu.make_async_copy(fine.at[0], fine_hbm.at[0], store_sem.at[2])
-    store_even.start()
 
     for copy in copies_a + copies_b + copies_c + copies_x + [copy_h1, copy_h2]:
         copy.wait_send()
-    store_odd.wait()
-    store_coarse.wait()
-    store_even.wait()
 
 
 def tables(slabs, n_pen, nx, nz):
@@ -448,15 +438,16 @@
     part = nx // GROUP
     at, fixed, left, ends, table = tables(slabs, n_pen, nx, nz)
     anywhere = pl.BlockSpec(memory_space=pl.ANY)
+    vector = pl.BlockSpec(memory_space=pltpu.VMEM)
     dma = pltpu.SemaphoreType.DMA
     return pl.pallas_call(
         functools.partial(kernel, (slabs, n_pen, groups, nx, nz, at)),
         out_shape=(
-            jax.ShapeDtypeStruct(density.shape, F32),
-            jax.ShapeDtypeStruct((1, nz, nx), F32),
+            pltpu.VMEM(density.shape, F32),
+            pltpu.VMEM((1, nz, nx), F32),
         ),
-        in_specs=[pl.BlockSpec(memory_space=pltpu.HBM)] * 5,
-        out_specs=(anywhere, anywhere),
+        in_specs=[anywhere] * 5,
+        out_specs=(vector, vector),
         scratch_shapes=[
             pltpu.VMEM(density.shape, F32),
             pltpu.VMEM(fixed.shape, BF16),
@@ -475,10 +466,7 @@
             pltpu.VMEM((GROUP, part, nz), F32),
             pltpu.VMEM((STATE_ROWS, nz), F32),
             pltpu.VMEM((n_pen, STATE_ROWS, nz), F32),
-            pltpu.VMEM(density.shape, F32),
-            pltpu.VMEM((nz, nx), F32),
             dma((5,)),
-            dma((3,)),
             dma, dma, dma, dma,
             pltpu.SemaphoreType.REGULAR,
             dma((GROUP,)), dma((GROUP,)), dma((groups,)), dma((groups,)),
@@ -488,7 +476,7 @@
             collective_id=0, has_side_effects=True, vmem_limit_bytes=32 * 1024 * 1024
         ),
         name="decompose",
-    )(density, fixed, left, ends, table)
+    )(*[pltpu.with_memory_space_constraint(a, pltpu.HBM) for a in (density, fixed, left, ends, table)])
 
 
 def solution(mesh):

time: 44.1 us -> 38.1 us (0.86)
  local copies, waits for them, and re-layouts: 6.83 us -> 1.42 us
    unnamed x12 -> x2, local copies, waits for them, and re-layouts: 6.83 us -> 1.42 us
where the time goes in v2:
time: 38.1 us; the launch traced here: 38 us
  Pallas kernels  35.9 us (94%)
  local copies, waits for them, and re-layouts  1.42 us (4%)
  between operations  0.64 us (2%)
    pallas_call x1, Pallas kernels, per_device(): pl.pallas_call(functools.partial(kernel, (slabs, n_pen, groups, nx, nz, a...  35.9 us
    unnamed x2, local copies, waits for them, and re-layouts  1.42 us

profile of v2, /device:TPU:1, one launch (start us, length us, event | category | flops | bytes accessed | tf_op | source)
XLA Modules:
  0.0 38.0 jit_solution(8210319446259523342)
XLA Ops:
  0.6 35.9 %decompose.1 = (f32[2,256,256]{2,1,0:T(8,128)S(1)}, f32[1,128,128]{2,1,0:T(8,128)S(1)}) custom-call(f32[2,256,256]{2,1,0:T(8,128)} %u_hbm.1, bf16[5,256,128]{2,1,0:T(8,128)(2,1)} %constant.8.clone.fixed_hbm, bf16[8,2,272,256]{3,2,1,0:T(8,128)(2,1)} %constant.9.clone.left_hbm, f32[8,136,128]{2,1,0:T(8,128)} %constant.10.clone.ends_hbm, ...), custom_call_target="tpu_custom_call" | custom-call | tf_op jit(solution)/shard_map/decompose/pallas_call | solution.py:443
  36.5 0.8 %copy.9 = f32[2,256,256]{2,1,0:T(8,128)} copy(f32[2,256,256]{2,1,0:T(8,128)S(1)} %get-tuple-element.2) | data formatting | bytes 1048576
  37.3 0.6 %copy.10 = f32[1,128,128]{2,1,0:T(8,128)} copy(f32[1,128,128]{2,1,0:T(8,128)S(1)} %get-tuple-element.3) | data formatting | bytes 131072

commit v3 on v2

--- a/solution.py
+++ b/solution.py
@@ -140,13 +140,13 @@
 
 def kernel(
     sizes,
-    u_hbm, fixed_hbm, left_hbm, ends_hbm, table_hbm,
-    fine, coarse,
-    u, fixed, left, ends, table, coarse_t, halo_in, halo_out, next_c,
-    out_a, in_a, out_b, in_b, out_c, in_c, out_x, in_x,
+    u_hbm, left_hbm, pz_hbm, ends_hbm, table_hbm,
+    fine, coarse, select,
+    u, left, pz, ends, table, refine_x, refine_z, coarse_t, halo_in, halo_out, next_c,
+    out_a, in_a, out_s, in_s, out_b, in_b, out_c, in_c, out_x, in_x,
     load_sem,
     h1_send, h1_recv, h2_send, h2_recv,
-    onward, a_send, a_recv, b_send, b_recv, c_send, c_recv, x_send, x_recv,
+    onward, a_send, a_recv, s_send, s_recv, b_send, b_recv, c_send, c_recv, x_send, x_recv,
 ):
     slabs, n_pen, groups, nx, nz, at = sizes
     part = nx // GROUP
@@ -155,52 +155,86 @@
     g = s // GROUP
     m = lax.rem(s, GROUP)
 
-    loads = [
-        pltpu.make_async_copy(u_hbm, u, load_sem.at[0]),
-        pltpu.make_async_copy(fixed_hbm, fixed, load_sem.at[1]),
-        pltpu.make_async_copy(left_hbm.at[p], left, load_sem.at[2]),
-        pltpu.make_async_copy(ends_hbm.at[p], ends, load_sem.at[3]),
-        pltpu.make_async_copy(table_hbm, table, load_sem.at[4]),
-    ]
-    for load in loads:
-        load.start()
+    load_u0 = pltpu.make_async_copy(u_hbm.at[0], u.at[0], load_sem.at[0])
+    load_left = pltpu.make_async_copy(left_hbm.at[p], left, load_sem.at[1])
+    load_u1 = pltpu.make_async_copy(u_hbm.at[1], u.at[1], load_sem.at[2])
+    load_pz = pltpu.make_async_copy(pz_hbm, pz, load_sem.at[3])
+    load_ends = pltpu.make_async_copy(ends_hbm.at[p], ends, load_sem.at[4])
+    load_table = pltpu.make_async_copy(table_hbm, table, load_sem.at[5])
+    load_u0.start()
+    load_left.start()
 
     turns = groups // 2
     turn, side = lax.rem(g, turns), g // turns
 
+    def mirrored(member, at_turn):
+        there = 2 * at_turn // turns
+        return member + there * (GROUP - 2 - 2 * member + 2 * lax.rem(member, 2))
+
+    held = mirrored(m, turn)
+
     def group_at(ahead, flips):
         return lax.rem(side + flips, 2) * turns + lax.rem(turn + ahead, turns)
+
+    def partner(step):
+        group = group_at(*step)
+        return group, group * GROUP + mirrored(held, lax.rem(group, turns))
 
     steps = sorted(range(turns), key=lambda k: -min(k, turns - k))
     far_first = [(k, flips) for k in steps for flips in (1, 0) if (k, flips) != (0, 0)]
     near = [(k, flips) for k, flips in far_first if min(k, turns - k) <= 1]
     members = [(g * GROUP + lax.rem(m + k, GROUP), p) for k in range(1, GROUP)]
-    others = [(group_at(*step) * GROUP + m, p) for step in near]
+    others = [(partner(step)[1], p) for step in near]
     peers = [(s, lax.rem(p + k, n_pen)) for k in range(1, n_pen)]
     above = (lax.rem(s + 1, slabs), p)
     below = (lax.rem(s + slabs - 1, slabs), p)
     barrier = pltpu.get_barrier_semaphore()
-    greeted = others + peers + members + [above]
+    for device in members:
+        pl.semaphore_signal(barrier, inc=1, device_id=device, device_id_type=MESH)
+    for load in (load_u1, load_pz, load_ends, load_table):
+        load.start()
+    greeted = [above] + others + peers
     for device in greeted:
         pl.semaphore_signal(barrier, inc=1, device_id=device, device_id_type=MESH)
 
-    for load in loads:
-        load.wait()
-
+    def spread_matrix(m, weight):
+        row = lax.broadcasted_iota(jnp.int32, (2 * m, m), 0)
+        column = lax.broadcasted_iota(jnp.int32, (2 * m, m), 1)
+        return weight(row, row - 2 * column).astype(BF16)
+
+    def even(row, away):
+        return jnp.where(away == 0, 1.0, 0.0)
+
+    def inner(row, away):
+        return jnp.where(away == 0, 1.0, jnp.where(jnp.abs(away) == 1, 0.5, 0.0))
+
+    def ending(row, away):
+        return jnp.where((row == 2 * nz - 1) & (away == 1), 1.0, inner(row, away))
+
+    select[0] = spread_matrix(nz, even)
+    select[1] = spread_matrix(nx, even)
+    refine_x[...] = spread_matrix(nx, inner)
+    refine_z[...] = spread_matrix(nz, ending)
+    row = lax.broadcasted_iota(jnp.int32, (nx, 2 * nx), 0)
+    column = lax.broadcasted_iota(jnp.int32, (nx, 2 * nx), 1)
+    take_x = jnp.where(column == 2 * row, 1.0, 0.0).astype(BF16)
+
+    load_u0.wait()
+    load_left.wait()
     u0 = parts(u[0])
-    u1 = parts(u[1])
-    lx = (left[0, : nx + 16], left[1, : nx + 16])
-    select_x = left[0, nx + 16 :]
-    pz = (fixed[0], fixed[1])
-    select_z = fixed[2]
+    lx = (left[0], left[1])
     t0 = dot3(lx, u0, True)
-    tc = dot(select_x, u0[0], True) + dot(select_x, u0[1], True)
-    t1 = dot3(lx, u1, True)
-    y0 = dot3(parts(t0), pz)
-    y1 = dot3(parts(t1), pz)
-    tc = parts(tc)
-    c = dot(tc[0], select_z) + dot(tc[1], select_z)
+    tc = parts(dot(take_x, u0[0], True) + dot(take_x, u0[1], True))
+    load_u1.wait()
+    t1 = dot3(lx, parts(u[1]), True)
+    load_pz.wait()
+    to_z = (pz[0], pz[1])
+    y0 = dot3(parts(t0), to_z)
+    y1 = dot3(parts(t1), to_z)
+    c = dot(tc[0], select[0]) + dot(tc[1], select[0])
     coarse_t[:nx, :] = c
+    load_ends.wait()
+    load_table.wait()
 
     def pen(k):
         return table[groups + p, k]
@@ -225,24 +259,31 @@
     n1 = y1[nx + STATE_ROWS : nx + 2 * STATE_ROWS] + s1 * jnp.roll(czx_state, 2, 0)
     out_a[:, 0:part, :] = p0.reshape(GROUP, part, nz)
     out_a[:, part : 2 * part, :] = p1.reshape(GROUP, part, nz)
-    out_a[:, 2 * part :, :] = jnp.broadcast_to(
-        jnp.where(rows8 < 2, n0, n1)[None], (GROUP, STATE_ROWS, nz)
-    )
-    in_a[m] = out_a[m]
+    out_s[...] = jnp.where(rows8 < 2, n0, n1)[0:4]
+    in_a[m] = out_a[held]
+    in_s[m] = out_s[...]
     halo_out[...] = c[0:8, :]
 
-    pl.semaphore_wait(barrier, len(greeted))
+    pl.semaphore_wait(barrier, len(members) + len(greeted))
 
     copies_a = []
     for k in range(1, GROUP):
         to = lax.rem(m + k, GROUP)
         copy = pltpu.make_async_remote_copy(
-            src_ref=out_a.at[to], dst_ref=in_a.at[m], send_sem=a_send.at[k], recv_sem=a_recv.at[k],
+            src_ref=out_a.at[mirrored(to, turn)], dst_ref=in_a.at[m],
+            send_sem=a_send.at[k], recv_sem=a_recv.at[k],
             device_id=(g * GROUP + to, p), device_id_type=MESH,
         )
         copy.start()
         copies_a.append(copy)
-    behind = (group_at(turns - 1, 0) * GROUP + m, p)
+    for k in range(1, GROUP):
+        copy = pltpu.make_async_remote_copy(
+            src_ref=out_s, dst_ref=in_s.at[m], send_sem=s_send.at[k], recv_sem=s_recv.at[k],
+            device_id=(g * GROUP + lax.rem(m + k, GROUP), p), device_id_type=MESH,
+        )
+        copy.start()
+        copies_a.append(copy)
+    behind = (partner((turns - 1, 0))[1], p)
     pl.semaphore_signal(onward, inc=1, device_id=behind, device_id_type=MESH)
     copy_h1 = pltpu.make_async_remote_copy(
         src_ref=halo_out, dst_ref=halo_in, send_sem=h1_send, recv_sem=h1_recv,
@@ -266,10 +307,10 @@
 
     def interpolant(values, beyond):
         high, low = parts(values)
-        along_x = dot(fixed[3], high) + dot(fixed[3], low)
+        along_x = dot(refine_x[...], high) + dot(refine_x[...], low)
         along_x = along_x + jnp.where(fine_rows == 2 * nx - 1, 0.5 * beyond, 0.0)
         high, low = parts(along_x)
-        return dot(fixed[4], high, True) + dot(fixed[4], low, True)
+        return dot(refine_z[...], high, True) + dot(refine_z[...], low, True)
 
     zi = lax.broadcasted_iota(jnp.int32, (2 * nz, 2 * nx), 0)
     xi = lax.broadcasted_iota(jnp.int32, (2 * nz, 2 * nx), 1)
@@ -289,12 +330,12 @@
         return in_a[k // 2, (k % 2) * part : (k % 2 + 1) * part, :]
 
     def state(k):
-        return in_a[k, 2 * part :, :]
+        return in_s[k]
 
     def states(base):
         even = weigh(base, 2, GROUP, state)
         odd = weigh(base + 1, 2, GROUP, state)
-        return even + jnp.roll(odd, STATE_ROWS - 2, 0)
+        return jnp.concatenate([even[0:2] + odd[2:4]] * (STATE_ROWS // 2), 0)
 
     for way, base in ((0, at.to_later), (1, at.to_earlier)):
         out_b[way, :part, :] = weigh(base, 1, 2 * GROUP, plane)
@@ -302,11 +343,11 @@
     pl.semaphore_wait(onward, 1)
     copies_b = []
     for k, step in enumerate(far_first):
-        to = group_at(*step)
+        to, device = partner(step)
         copy = pltpu.make_async_remote_copy(
             src_ref=out_b.at[jnp.where(to > g, 0, 1)], dst_ref=in_b.at[g],
             send_sem=b_send.at[k], recv_sem=b_recv.at[k],
-            device_id=(to * GROUP + m, p), device_id_type=MESH,
+            device_id=(device, p), device_id_type=MESH,
         )
         copy.start()
         copies_b.append(copy)
@@ -350,12 +391,12 @@
     for k in range(1, GROUP):
         to = lax.rem(m + k, GROUP)
         copy = pltpu.make_async_remote_copy(
-            src_ref=out_c.at[to], dst_ref=in_c.at[m], send_sem=c_send.at[k], recv_sem=c_recv.at[k],
+            src_ref=out_c.at[to], dst_ref=in_c.at[held], send_sem=c_send.at[k], recv_sem=c_recv.at[k],
             device_id=(g * GROUP + to, p), device_id_type=MESH,
         )
         copy.start()
         copies_c.append(copy)
-    in_c[m] = out_c[m]
+    in_c[held] = out_c[m]
     in_x[p] = out_x[...]
 
     for copy in copies_x:
@@ -368,15 +409,25 @@
     rest = rest + ends[:nx, 0:1] * x_earlier + ends[:nx, 1:2] * x_later
     for copy in copies_c:
         copy.wait_recv()
-    values = (in_c[...].reshape(nx, nz) + rest).T
-    coarse[0] = values
-    high, low = parts(values)
-    spread = dot(select_z, high) + dot(select_z, low)
-    high, low = parts(spread)
-    fine[0] = fine[0] + dot(high, select_x) + dot(low, select_x)
+    coarse[...] = (in_c[...].reshape(nx, nz) + rest).T
 
     for copy in copies_a + copies_b + copies_c + copies_x + [copy_h1, copy_h2]:
         copy.wait_send()
+
+
+def finish(part, coarse, select, fine_hbm, coarse_hbm, even, sem):
+    odd_out = pltpu.make_async_copy(part.at[1], fine_hbm.at[1], sem.at[0])
+    coarse_out = pltpu.make_async_copy(coarse, coarse_hbm.at[0], sem.at[1])
+    odd_out.start()
+    coarse_out.start()
+    high, low = parts(coarse[...])
+    high, low = parts(dot(select[0], high) + dot(select[0], low))
+    even[...] = part[0] + dot(high, select[1], True) + dot(low, select[1], True)
+    even_out = pltpu.make_async_copy(even, fine_hbm.at[0], sem.at[2])
+    even_out.start()
+    odd_out.wait()
+    coarse_out.wait()
+    even_out.wait()
 
 
 def tables(slabs, n_pen, nx, nz):
@@ -385,16 +436,8 @@
     by = Blocks(slabs, groups)
     bz = Blocks(nz, 1)
 
-    pz_high, pz_low = split(bz.diagonal[0].T)
-    select = np.zeros((2 * nz, nz))
-    select[2 * np.arange(nz), np.arange(nz)] = 1.0
-    inner = refine_matrix(nx)
-    inner[2 * nx - 1, nx - 1] = 0.5
-    fixed = np.stack(
-        [pz_high, pz_low, split(select)[0], split(inner)[0], split(refine_matrix(nz))[0]]
-    )
-
-    left = np.zeros((n_pen, 2, 2 * nx + 16, 2 * nx), ml_dtypes.bfloat16)
+    pz = np.stack(split(bz.diagonal[0].T))
+    left = np.zeros((n_pen, 2, nx + 16, 2 * nx), ml_dtypes.bfloat16)
     inverse = inverse_mass(nz)
     ends = np.zeros((n_pen, nx + 8, nz), np.float32)
     ends[:, nx] = inverse[:, 0] / 3.0
@@ -404,9 +447,7 @@
         states = np.zeros((16, 2 * nx))
         states[0] = states[10] = bx.to_later[b]
         states[1] = states[11] = bx.to_earlier[b]
-        block = split(np.concatenate([bx.diagonal[b], states]))
-        left[b, 0, : nx + 16], left[b, 1, : nx + 16] = block
-        left[b, 0, nx + 16 + np.arange(nx), 2 * np.arange(nx)] = 1.0
+        left[b, 0], left[b, 1] = split(np.concatenate([bx.diagonal[b], states]))
         ends[b, :nx, 0] = bx.falling[b]
         ends[b, :nx, 1] = bx.rising[b]
         pens[b, :n_pen] = bx.from_earlier[b]
@@ -429,54 +470,73 @@
         table[b, at.rising : at.from_earlier] = by.rising[b]
         table[b, at.from_earlier : at.from_later] = by.from_earlier[b]
         table[b, at.from_later :] = by.from_later[b]
-    return at, fixed, left, ends, table
+    return at, left, pz, ends, table
 
 
 def per_device(slabs, n_pen, density):
     nz, nx = density.shape[1] // 2, density.shape[2] // 2
     groups = slabs // GROUP
     part = nx // GROUP
-    at, fixed, left, ends, table = tables(slabs, n_pen, nx, nz)
+    at, *operands = tables(slabs, n_pen, nx, nz)
+    left, pz, ends, table = operands
+    operands = [pltpu.with_memory_space_constraint(a, pltpu.HBM) for a in (density, *operands)]
     anywhere = pl.BlockSpec(memory_space=pl.ANY)
     vector = pl.BlockSpec(memory_space=pltpu.VMEM)
     dma = pltpu.SemaphoreType.DMA
-    return pl.pallas_call(
+    spread = (2 * nz, nz), (2 * nx, nx)
+
+    def tile(*shape):
+        return pltpu.VMEM(shape, F32)
+
+    partial, coarse, select = pl.pallas_call(
         functools.partial(kernel, (slabs, n_pen, groups, nx, nz, at)),
         out_shape=(
-            pltpu.VMEM(density.shape, F32),
-            pltpu.VMEM((1, nz, nx), F32),
+            tile(*density.shape),
+            tile(nz, nx),
+            pltpu.VMEM((2, 2 * nz, nz), BF16),
         ),
         in_specs=[anywhere] * 5,
-        out_specs=(vector, vector),
+        out_specs=(vector, vector, vector),
         scratch_shapes=[
-            pltpu.VMEM(density.shape, F32),
-            pltpu.VMEM(fixed.shape, BF16),
+            tile(*density.shape),
             pltpu.VMEM(left.shape[1:], BF16),
-            pltpu.VMEM(ends.shape[1:], F32),
+            pltpu.VMEM(pz.shape, BF16),
+            tile(*ends.shape[1:]),
             pltpu.SMEM(table.shape, F32),
-            pltpu.VMEM((nx + 8, nz), F32),
-            pltpu.VMEM((8, nz), F32),
-            pltpu.VMEM((8, nz), F32),
-            pltpu.VMEM((nx + 8, nz), F32),
-            pltpu.VMEM((GROUP, 2 * part + STATE_ROWS, nz), F32),
-            pltpu.VMEM((GROUP, 2 * part + STATE_ROWS, nz), F32),
-            pltpu.VMEM((2, part + STATE_ROWS, nz), F32),
-            pltpu.VMEM((groups, part + STATE_ROWS, nz), F32),
-            pltpu.VMEM((GROUP, part, nz), F32),
-            pltpu.VMEM((GROUP, part, nz), F32),
-            pltpu.VMEM((STATE_ROWS, nz), F32),
-            pltpu.VMEM((n_pen, STATE_ROWS, nz), F32),
-            dma((5,)),
+            pltpu.VMEM(spread[1], BF16),
+            pltpu.VMEM(spread[0], BF16),
+            tile(nx + 8, nz),
+            tile(8, nz), tile(8, nz),
+            tile(nx + 8, nz),
+            tile(GROUP, 2 * part, nz), tile(GROUP, 2 * part, nz),
+            tile(4, nz), tile(GROUP, 4, nz),
+            tile(2, part + STATE_ROWS, nz), tile(groups, part + STATE_ROWS, nz),
+            tile(GROUP, part, nz), tile(GROUP, part, nz),
+            tile(STATE_ROWS, nz), tile(n_pen, STATE_ROWS, nz),
+            dma((6,)),
             dma, dma, dma, dma,
             pltpu.SemaphoreType.REGULAR,
-            dma((GROUP,)), dma((GROUP,)), dma((groups,)), dma((groups,)),
+            dma((GROUP,)), dma((GROUP,)), dma((GROUP,)), dma((GROUP,)),
+            dma((groups,)), dma((groups,)),
             dma((GROUP,)), dma((GROUP,)), dma((n_pen,)), dma((n_pen,)),
         ],
         compiler_params=pltpu.CompilerParams(
             collective_id=0, has_side_effects=True, vmem_limit_bytes=32 * 1024 * 1024
         ),
         name="decompose",
-    )(*[pltpu.with_memory_space_constraint(a, pltpu.HBM) for a in (density, fixed, left, ends, table)])
+    )(*operands)
+    return pl.pallas_call(
+        finish,
+        out_shape=(
+            jax.ShapeDtypeStruct(density.shape, F32),
+            jax.ShapeDtypeStruct((1, nz, nx), F32),
+        ),
+        in_specs=[vector] * 3,
+        out_specs=(anywhere, anywhere),
+        scratch_shapes=[tile(2 * nz, 2 * nx), dma((3,))],
+        compiler_params=pltpu.CompilerParams(vmem_limit_bytes=16 * 1024 * 1024),
+        name="finish",
+    )(partial, coarse, select)
 
 
 def solution(mesh):

time: 38.1 us -> 36 us (0.945)
  local copies, waits for them, and re-layouts: 1.42 us -> 0 us
  Pallas kernels: 35.9 us -> 35.2 us
    pallas_call x1, Pallas kernels: 35.9 us -> 34.1 us  [per_device(): pl.pallas_call(functools.partial(kernel, (slabs, n_pen, groups, nx, nz, a...]
    unnamed x2 -> x0, local copies, waits for them, and re-layouts: 1.42 us -> none
    pallas_call x0 -> x1, Pallas kernels: none -> 1.13 us  [per_device(): pl.pallas_call(finish, out_shape=(jax.ShapeDtypeStruct(density.shape, F32...]
where the time goes in v3:
time: 36 us; the launch traced here: 35.9 us
  Pallas kernels  35.2 us (98%)
  between operations  0.64 us (2%)
    pallas_call x1, Pallas kernels, per_device(): pl.pallas_call(functools.partial(kernel, (slabs, n_pen, groups, nx, nz, a...  34.1 us
    pallas_call x1, Pallas kernels, per_device(): pl.pallas_call(finish, out_shape=(jax.ShapeDtypeStruct(density.shape, F32...  1.13 us

profile of v3, /device:TPU:1, one launch (start us, length us, event | category | flops | bytes accessed | tf_op | source)
XLA Modules:
  0.0 35.9 jit_solution(911950681789491872)
XLA Ops:
  0.6 34.1 %decompose.1 = (f32[2,256,256]{2,1,0:T(8,128)S(1)}, f32[128,128]{1,0:T(8,128)S(1)}, bf16[2,256,128]{2,1,0:T(8,128)(2,1)S(1)}) custom-call(f32[2,256,256]{2,1,0:T(8,128)} %u_hbm.1, bf16[8,2,144,256]{3,2,1,0:T(8,128)(2,1)} %constant.8.clone.left_hbm, bf16[2,256,128]{2,1,0:T(8,128)(2,1)} %constant.9.clone.pz_hbm, f32[8,136,128]{2,1,0:T(8,128)} %constant.10.clone.ends_hbm, ...), custom_call_target="tpu_custom_call" | custom-call | tf_op jit(solution)/shard_map/decompose/pallas_call | solution.py:491
  34.7 1.1 %finish.1 = (f32[2,256,256]{2,1,0:T(8,128)}, f32[1,128,128]{2,1,0:T(8,128)}) custom-call(f32[2,256,256]{2,1,0:T(8,128)S(1)} %get-tuple-element.5.part, f32[128,128]{1,0:T(8,128)S(1)} %get-tuple-element.6.coarse, bf16[2,256,128]{2,1,0:T(8,128)(2,1)S(1)} %get-tuple-element.7.select), custom_call_target="tpu_custom_call" | custom-call | tf_op jit(solution)/shard_map/finish/pallas_call | solution.py:528

commit v4 on v3

--- a/solution.py
+++ b/solution.py
@@ -146,7 +146,7 @@
     out_a, in_a, out_s, in_s, out_b, in_b, out_c, in_c, out_x, in_x,
     load_sem,
     h1_send, h1_recv, h2_send, h2_recv,
-    onward, a_send, a_recv, s_send, s_recv, b_send, b_recv, c_send, c_recv, x_send, x_recv,
+    onward, along, across, a_send, a_recv, s_send, s_recv, b_send, b_recv, c_send, c_recv, x_send, x_recv,
 ):
     slabs, n_pen, groups, nx, nz, at = sizes
     part = nx // GROUP
@@ -185,7 +185,14 @@
     near = [(k, flips) for k, flips in far_first if min(k, turns - k) <= 1]
     members = [(g * GROUP + lax.rem(m + k, GROUP), p) for k in range(1, GROUP)]
     others = [(partner(step)[1], p) for step in near]
-    peers = [(s, lax.rem(p + k, n_pen)) for k in range(1, n_pen)]
+    around = n_pen // 2
+    ring, place = p // around, lax.rem(p, around)
+
+    def pen_at(ahead, flips):
+        return lax.rem(ring + flips, 2) * around + lax.rem(place + ahead, around)
+
+    next_pen, previous_pen, across_pen = pen_at(1, 0), pen_at(around - 1, 0), pen_at(0, 1)
+    peers = [(s, q) for q in (across_pen, next_pen, previous_pen)]
     above = (lax.rem(s + 1, slabs), p)
     below = (lax.rem(s + slabs - 1, slabs), p)
     barrier = pltpu.get_barrier_semaphore()
@@ -285,37 +292,12 @@
         copies_a.append(copy)
     behind = (partner((turns - 1, 0))[1], p)
     pl.semaphore_signal(onward, inc=1, device_id=behind, device_id_type=MESH)
-    copy_h1 = pltpu.make_async_remote_copy(
-        src_ref=halo_out, dst_ref=halo_in, send_sem=h1_send, recv_sem=h1_recv,
-        device_id=(s, lax.rem(p + n_pen - 1, n_pen)), device_id_type=MESH,
-    )
-    copy_h1.start()
-
+    pl.semaphore_signal(along, inc=1, device_id=(s, previous_pen), device_id_type=MESH)
     in_b[g] = jnp.zeros((part + STATE_ROWS, nz), F32)
     rest = d - ex
 
-    copy_h1.wait_recv()
-    halo = jnp.where(p == n_pen - 1, c[nx - 1 : nx, :], halo_in[0:1, :])
-    coarse_t[nx : nx + 8, :] = jnp.broadcast_to(halo, (8, nz))
-    copy_h2 = pltpu.make_async_remote_copy(
-        src_ref=coarse_t, dst_ref=next_c, send_sem=h2_send, recv_sem=h2_recv,
-        device_id=below, device_id_type=MESH,
-    )
-    copy_h2.start()
-
-    fine_rows = lax.broadcasted_iota(jnp.int32, (2 * nx, nz), 0)
-
-    def interpolant(values, beyond):
-        high, low = parts(values)
-        along_x = dot(refine_x[...], high) + dot(refine_x[...], low)
-        along_x = along_x + jnp.where(fine_rows == 2 * nx - 1, 0.5 * beyond, 0.0)
-        high, low = parts(along_x)
-        return dot(refine_z[...], high, True) + dot(refine_z[...], low, True)
-
-    zi = lax.broadcasted_iota(jnp.int32, (2 * nz, 2 * nx), 0)
-    xi = lax.broadcasted_iota(jnp.int32, (2 * nz, 2 * nx), 1)
-    kept = ((zi | xi) & 1) == 0
-    fine[0] = jnp.where(kept, 0.0, u[0] - interpolant(c, halo))
+    pl.semaphore_wait(along, 1)
+    pl.semaphore_signal(across, inc=1, device_id=(s, across_pen), device_id_type=MESH)
 
     for copy in copies_a:
         copy.wait_recv()
@@ -352,15 +334,25 @@
         copy.start()
         copies_b.append(copy)
 
+    pl.semaphore_wait(across, 1)
+    copy_h1 = pltpu.make_async_remote_copy(
+        src_ref=halo_out, dst_ref=halo_in, send_sem=h1_send, recv_sem=h1_recv,
+        device_id=(s, lax.rem(p + n_pen - 1, n_pen)), device_id_type=MESH,
+    )
+    copy_h1.start()
+
     for i in range(GROUP):
         out_c[i] = weigh(at.local + 2 * GROUP * i, 1, 2 * GROUP, plane)
     own_states = states(at.local + 2 * GROUP * m)
 
-    copy_h2.wait_recv()
-    last = s == slabs - 1
-    after = jnp.where(last, coarse_t[...], next_c[...])
-    middle = 0.5 * (coarse_t[...] + after)
-    fine[1] = u[1] - interpolant(middle[:nx], middle[nx : nx + 1])
+    copy_h1.wait_recv()
+    halo = jnp.where(p == n_pen - 1, c[nx - 1 : nx, :], halo_in[0:1, :])
+    coarse_t[nx : nx + 8, :] = jnp.broadcast_to(halo, (8, nz))
+    copy_h2 = pltpu.make_async_remote_copy(
+        src_ref=coarse_t, dst_ref=next_c, send_sem=h2_send, recv_sem=h2_recv,
+        device_id=below, device_id_type=MESH,
+    )
+    copy_h2.start()
 
     for copy in copies_b:
         copy.wait_recv()
@@ -398,6 +390,26 @@
         copies_c.append(copy)
     in_c[held] = out_c[m]
     in_x[p] = out_x[...]
+
+    fine_rows = lax.broadcasted_iota(jnp.int32, (2 * nx, nz), 0)
+
+    def interpolant(values, beyond):
+        high, low = parts(values)
+        along_x = dot(refine_x[...], high) + dot(refine_x[...], low)
+        along_x = along_x + jnp.where(fine_rows == 2 * nx - 1, 0.5 * beyond, 0.0)
+        high, low = parts(along_x)
+        return dot(refine_z[...], high, True) + dot(refine_z[...], low, True)
+
+    zi = lax.broadcasted_iota(jnp.int32, (2 * nz, 2 * nx), 0)
+    xi = lax.broadcasted_iota(jnp.int32, (2 * nz, 2 * nx), 1)
+    kept = ((zi | xi) & 1) == 0
+    fine[0] = jnp.where(kept, 0.0, u[0] - interpolant(c, halo))
+
+    copy_h2.wait_recv()
+    last = s == slabs - 1
+    after = jnp.where(last, coarse_t[...], next_c[...])
+    middle = 0.5 * (coarse_t[...] + after)
+    fine[1] = u[1] - interpolant(middle[:nx], middle[nx : nx + 1])
 
     for copy in copies_x:
         copy.wait_recv()
@@ -515,7 +527,7 @@
             tile(STATE_ROWS, nz), tile(n_pen, STATE_ROWS, nz),
             dma((6,)),
             dma, dma, dma, dma,
-            pltpu.SemaphoreType.REGULAR,
+            *[pltpu.SemaphoreType.REGULAR] * 3,
             dma((GROUP,)), dma((GROUP,)), dma((GROUP,)), dma((GROUP,)),
             dma((groups,)), dma((groups,)),
             dma((GROUP,)), dma((GROUP,)), dma((n_pen,)), dma((n_pen,)),

time: 36 us -> 35.5 us (0.986)
  Pallas kernels: 35.2 us -> 34.8 us
    pallas_call x1, Pallas kernels: 34.1 us -> 33.6 us  [per_device(): pl.pallas_call(functools.partial(kernel, (slabs, n_pen, groups, nx, nz, a...]
where the time goes in v4:
time: 35.5 us; the launch traced here: 35.4 us
  Pallas kernels  34.8 us (98%)
  between operations  0.64 us (2%)
    pallas_call x1, Pallas kernels, per_device(): pl.pallas_call(functools.partial(kernel, (slabs, n_pen, groups, nx, nz, a...  33.6 us
    pallas_call x1, Pallas kernels, per_device(): pl.pallas_call(finish, out_shape=(jax.ShapeDtypeStruct(density.shape, F32...  1.13 us

profile of v4, /device:TPU:1, one launch (start us, length us, event | category | flops | bytes accessed | tf_op | source)
XLA Modules:
  0.0 35.4 jit_solution(15264180541482772375)
XLA Ops:
  0.6 33.6 %decompose.1 = (f32[2,256,256]{2,1,0:T(8,128)S(1)}, f32[128,128]{1,0:T(8,128)S(1)}, bf16[2,256,128]{2,1,0:T(8,128)(2,1)S(1)}) custom-call(f32[2,256,256]{2,1,0:T(8,128)} %u_hbm.1, bf16[8,2,144,256]{3,2,1,0:T(8,128)(2,1)} %constant.8.clone.left_hbm, bf16[2,256,128]{2,1,0:T(8,128)(2,1)} %constant.9.clone.pz_hbm, f32[8,136,128]{2,1,0:T(8,128)} %constant.10.clone.ends_hbm, ...), custom_call_target="tpu_custom_call" | custom-call | tf_op jit(solution)/shard_map/decompose/pallas_call | solution.py:503
  34.3 1.1 %finish.1 = (f32[2,256,256]{2,1,0:T(8,128)}, f32[1,128,128]{2,1,0:T(8,128)}) custom-call(f32[2,256,256]{2,1,0:T(8,128)S(1)} %get-tuple-element.5.part, f32[128,128]{1,0:T(8,128)S(1)} %get-tuple-element.6.coarse, bf16[2,256,128]{2,1,0:T(8,128)(2,1)S(1)} %get-tuple-element.7.select), custom_call_target="tpu_custom_call" | custom-call | tf_op jit(solution)/shard_map/finish/pallas_call | solution.py:540

commit v5 on v4

--- a/solution.py
+++ b/solution.py
@@ -143,10 +143,11 @@
     u_hbm, left_hbm, pz_hbm, ends_hbm, table_hbm,
     fine, coarse, select,
     u, left, pz, ends, table, refine_x, refine_z, coarse_t, halo_in, halo_out, next_c,
-    out_a, in_a, out_s, in_s, out_b, in_b, out_c, in_c, out_x, in_x,
+    out_a, in_a, out_s, in_s, out_b, in_b, out_t, in_t, out_c, in_c, out_x, in_x,
+    x_falling, x_rising,
     load_sem,
     h1_send, h1_recv, h2_send, h2_recv,
-    onward, along, across, a_send, a_recv, s_send, s_recv, b_send, b_recv, c_send, c_recv, x_send, x_recv,
+    onward, along, across, a_send, a_recv, s_send, s_recv, b_send, b_recv, t_send, t_recv, c_send, c_recv, x_send, x_recv,
 ):
     slabs, n_pen, groups, nx, nz, at = sizes
     part = nx // GROUP
@@ -192,6 +193,8 @@
         return lax.rem(ring + flips, 2) * around + lax.rem(place + ahead, around)
 
     next_pen, previous_pen, across_pen = pen_at(1, 0), pen_at(around - 1, 0), pen_at(0, 1)
+    around_first = sorted(range(around), key=lambda k: -min(k, around - k))
+    far_pens = [(k, flips) for flips in (1, 0) for k in around_first if (k, flips) != (0, 0)]
     peers = [(s, q) for q in (across_pen, next_pen, previous_pen)]
     above = (lax.rem(s + 1, slabs), p)
     below = (lax.rem(s + slabs - 1, slabs), p)
@@ -273,7 +276,14 @@
 
     pl.semaphore_wait(barrier, len(members) + len(greeted))
 
-    copies_a = []
+    copies_s, copies_a = [], []
+    for k in range(1, GROUP):
+        copy = pltpu.make_async_remote_copy(
+            src_ref=out_s, dst_ref=in_s.at[m], send_sem=s_send.at[k], recv_sem=s_recv.at[k],
+            device_id=(g * GROUP + lax.rem(m + k, GROUP), p), device_id_type=MESH,
+        )
+        copy.start()
+        copies_s.append(copy)
     for k in range(1, GROUP):
         to = lax.rem(m + k, GROUP)
         copy = pltpu.make_async_remote_copy(
@@ -283,24 +293,17 @@
         )
         copy.start()
         copies_a.append(copy)
-    for k in range(1, GROUP):
-        copy = pltpu.make_async_remote_copy(
-            src_ref=out_s, dst_ref=in_s.at[m], send_sem=s_send.at[k], recv_sem=s_recv.at[k],
-            device_id=(g * GROUP + lax.rem(m + k, GROUP), p), device_id_type=MESH,
-        )
-        copy.start()
-        copies_a.append(copy)
     behind = (partner((turns - 1, 0))[1], p)
     pl.semaphore_signal(onward, inc=1, device_id=behind, device_id_type=MESH)
     pl.semaphore_signal(along, inc=1, device_id=(s, previous_pen), device_id_type=MESH)
-    in_b[g] = jnp.zeros((part + STATE_ROWS, nz), F32)
+    in_b[g] = jnp.zeros((part, nz), F32)
+    in_t[g] = jnp.zeros((2, nz), F32)
     rest = d - ex
+    x_falling[...] = jnp.broadcast_to(ends[:nx, 0:1], (nx, nz))
+    x_rising[...] = jnp.broadcast_to(ends[:nx, 1:2], (nx, nz))
 
     pl.semaphore_wait(along, 1)
     pl.semaphore_signal(across, inc=1, device_id=(s, across_pen), device_id_type=MESH)
-
-    for copy in copies_a:
-        copy.wait_recv()
 
     def weigh(base, step, count, get):
         total = table[g, base] * get(0)
@@ -311,28 +314,37 @@
     def plane(k):
         return in_a[k // 2, (k % 2) * part : (k % 2 + 1) * part, :]
 
-    def state(k):
-        return in_s[k]
-
     def states(base):
-        even = weigh(base, 2, GROUP, state)
-        odd = weigh(base + 1, 2, GROUP, state)
-        return jnp.concatenate([even[0:2] + odd[2:4]] * (STATE_ROWS // 2), 0)
-
-    for way, base in ((0, at.to_later), (1, at.to_earlier)):
-        out_b[way, :part, :] = weigh(base, 1, 2 * GROUP, plane)
-        out_b[way, part:, :] = states(base)
+        even = weigh(base, 2, GROUP, lambda k: in_s[k])
+        odd = weigh(base + 1, 2, GROUP, lambda k: in_s[k])
+        return even[0:2] + odd[2:4]
+
+    def to_groups(source, landing, send_sem, recv_sem):
+        copies = []
+        for k, step in enumerate(far_first):
+            to, device = partner(step)
+            copy = pltpu.make_async_remote_copy(
+                src_ref=source.at[jnp.where(to > g, 0, 1)], dst_ref=landing.at[g],
+                send_sem=send_sem.at[k], recv_sem=recv_sem.at[k],
+                device_id=(device, p), device_id_type=MESH,
+            )
+            copy.start()
+            copies.append(copy)
+        return copies
+
+    for copy in copies_s:
+        copy.wait_recv()
+    out_t[0] = states(at.to_later)
+    out_t[1] = states(at.to_earlier)
     pl.semaphore_wait(onward, 1)
-    copies_b = []
-    for k, step in enumerate(far_first):
-        to, device = partner(step)
-        copy = pltpu.make_async_remote_copy(
-            src_ref=out_b.at[jnp.where(to > g, 0, 1)], dst_ref=in_b.at[g],
-            send_sem=b_send.at[k], recv_sem=b_recv.at[k],
-            device_id=(device, p), device_id_type=MESH,
-        )
-        copy.start()
-        copies_b.append(copy)
+    copies_t = to_groups(out_t, in_t, t_send, t_recv)
+    own_states = states(at.local + 2 * GROUP * m)
+
+    for copy in copies_a:
+        copy.wait_recv()
+    out_b[0] = weigh(at.to_later, 1, 2 * GROUP, plane)
+    out_b[1] = weigh(at.to_earlier, 1, 2 * GROUP, plane)
+    copies_b = to_groups(out_b, in_b, b_send, b_recv)
 
     pl.semaphore_wait(across, 1)
     copy_h1 = pltpu.make_async_remote_copy(
@@ -343,7 +355,25 @@
 
     for i in range(GROUP):
         out_c[i] = weigh(at.local + 2 * GROUP * i, 1, 2 * GROUP, plane)
-    own_states = states(at.local + 2 * GROUP * m)
+
+    for copy in copies_t:
+        copy.wait_recv()
+    own_states = (
+        own_states
+        + table[g, at.falling + m] * weigh(at.from_earlier, 1, groups, lambda k: in_t[k])
+        + table[g, at.rising + m] * weigh(at.from_later, 1, groups, lambda k: in_t[k])
+        - czx_state[0:2]
+    )
+    out_x[...] = own_states
+    in_x[p] = own_states
+    copies_x = []
+    for k, step in enumerate(far_pens):
+        copy = pltpu.make_async_remote_copy(
+            src_ref=out_x, dst_ref=in_x.at[p], send_sem=x_send.at[k], recv_sem=x_recv.at[k],
+            device_id=(s, pen_at(*step)), device_id_type=MESH,
+        )
+        copy.start()
+        copies_x.append(copy)
 
     copy_h1.wait_recv()
     halo = jnp.where(p == n_pen - 1, c[nx - 1 : nx, :], halo_in[0:1, :])
@@ -358,26 +388,11 @@
         copy.wait_recv()
     from_earlier = weigh(at.from_earlier, 1, groups, lambda k: in_b[k])
     from_later = weigh(at.from_later, 1, groups, lambda k: in_b[k])
-    own_states = (
-        own_states
-        + table[g, at.falling + m] * from_earlier[part:]
-        + table[g, at.rising + m] * from_later[part:]
-        - czx_state
-    )
-    out_x[...] = own_states
-    copies_x = []
-    for k in range(1, n_pen):
-        copy = pltpu.make_async_remote_copy(
-            src_ref=out_x, dst_ref=in_x.at[p], send_sem=x_send.at[k], recv_sem=x_recv.at[k],
-            device_id=(s, lax.rem(p + k, n_pen)), device_id_type=MESH,
-        )
-        copy.start()
-        copies_x.append(copy)
     for i in range(GROUP):
         out_c[i] = (
             out_c[i]
-            + table[g, at.falling + i] * from_earlier[:part]
-            + table[g, at.rising + i] * from_later[:part]
+            + table[g, at.falling + i] * from_earlier
+            + table[g, at.rising + i] * from_later
         )
     copies_c = []
     for k in range(1, GROUP):
@@ -389,7 +404,6 @@
         copy.start()
         copies_c.append(copy)
     in_c[held] = out_c[m]
-    in_x[p] = out_x[...]
 
     fine_rows = lax.broadcasted_iota(jnp.int32, (2 * nx, nz), 0)
 
@@ -411,6 +425,8 @@
     middle = 0.5 * (coarse_t[...] + after)
     fine[1] = u[1] - interpolant(middle[:nx], middle[nx : nx + 1])
 
+    for copy in copies_s + copies_a + copies_t + copies_b + copies_x + copies_c + [copy_h1, copy_h2]:
+        copy.wait_send()
     for copy in copies_x:
         copy.wait_recv()
     x_earlier = pen(0) * in_x[0, 0:1, :]
@@ -418,13 +434,10 @@
     for k in range(1, n_pen):
         x_earlier = x_earlier + pen(k) * in_x[k, 0:1, :]
         x_later = x_later + pen(n_pen + k) * in_x[k, 1:2, :]
-    rest = rest + ends[:nx, 0:1] * x_earlier + ends[:nx, 1:2] * x_later
+    rest = rest + x_falling[...] * x_earlier + x_rising[...] * x_later
     for copy in copies_c:
         copy.wait_recv()
     coarse[...] = (in_c[...].reshape(nx, nz) + rest).T
-
-    for copy in copies_a + copies_b + copies_c + copies_x + [copy_h1, copy_h2]:
-        copy.wait_send()
 
 
 def finish(part, coarse, select, fine_hbm, coarse_hbm, even, sem):
@@ -522,14 +535,16 @@
             tile(nx + 8, nz),
             tile(GROUP, 2 * part, nz), tile(GROUP, 2 * part, nz),
             tile(4, nz), tile(GROUP, 4, nz),
-            tile(2, part + STATE_ROWS, nz), tile(groups, part + STATE_ROWS, nz),
+            tile(2, part, nz), tile(groups, part, nz),
+            tile(2, 2, nz), tile(groups, 2, nz),
             tile(GROUP, part, nz), tile(GROUP, part, nz),
-            tile(STATE_ROWS, nz), tile(n_pen, STATE_ROWS, nz),
+            tile(2, nz), tile(n_pen, 2, nz),
+            tile(nx, nz), tile(nx, nz),
             dma((6,)),
             dma, dma, dma, dma,
             *[pltpu.SemaphoreType.REGULAR] * 3,
             dma((GROUP,)), dma((GROUP,)), dma((GROUP,)), dma((GROUP,)),
-            dma((groups,)), dma((groups,)),
+            dma((groups,)), dma((groups,)), dma((groups,)), dma((groups,)),
             dma((GROUP,)), dma((GROUP,)), dma((n_pen,)), dma((n_pen,)),
         ],
         compiler_params=pltpu.CompilerParams(

time: 35.5 us -> 33.1 us (0.932)
  Pallas kernels: 34.8 us -> 32.3 us
    pallas_call x1, Pallas kernels: 33.6 us -> 31.2 us  [per_device(): pl.pallas_call(functools.partial(kernel, (slabs, n_pen, groups, nx, nz, a...]
where the time goes in v5:
time: 33.1 us; the launch traced here: 33 us
  Pallas kernels  32.3 us (98%)
  between operations  0.64 us (2%)
    pallas_call x1, Pallas kernels, per_device(): pl.pallas_call(functools.partial(kernel, (slabs, n_pen, groups, nx, nz, a...  31.2 us
    pallas_call x1, Pallas kernels, per_device(): pl.pallas_call(finish, out_shape=(jax.ShapeDtypeStruct(density.shape, F32...  1.13 us

profile of v5, /device:TPU:1, one launch (start us, length us, event | category | flops | bytes accessed | tf_op | source)
XLA Modules:
  0.0 33.0 jit_solution(11864966016160263667)
XLA Ops:
  0.6 31.2 %decompose.1 = (f32[2,256,256]{2,1,0:T(8,128)S(1)}, f32[128,128]{1,0:T(8,128)S(1)}, bf16[2,256,128]{2,1,0:T(8,128)(2,1)S(1)}) custom-call(f32[2,256,256]{2,1,0:T(8,128)} %u_hbm.1, bf16[8,2,144,256]{3,2,1,0:T(8,128)(2,1)} %constant.8.clone.left_hbm, bf16[2,256,128]{2,1,0:T(8,128)(2,1)} %constant.9.clone.pz_hbm, f32[8,136,128]{2,1,0:T(8,128)} %constant.10.clone.ends_hbm, ...), custom_call_target="tpu_custom_call" | custom-call | tf_op jit(solution)/shard_map/decompose/pallas_call | solution.py:516
  31.8 1.1 %finish.1 = (f32[2,256,256]{2,1,0:T(8,128)}, f32[1,128,128]{2,1,0:T(8,128)}) custom-call(f32[2,256,256]{2,1,0:T(8,128)S(1)} %get-tuple-element.5.part, f32[128,128]{1,0:T(8,128)S(1)} %get-tuple-element.6.coarse, bf16[2,256,128]{2,1,0:T(8,128)(2,1)S(1)} %get-tuple-element.7.select), custom_call_target="tpu_custom_call" | custom-call | tf_op jit(solution)/shard_map/finish/pallas_call | solution.py:555

commit v6 on v5

--- a/solution.py
+++ b/solution.py
@@ -147,7 +147,7 @@
     x_falling, x_rising,
     load_sem,
     h1_send, h1_recv, h2_send, h2_recv,
-    onward, along, across, a_send, a_recv, s_send, s_recv, b_send, b_recv, t_send, t_recv, c_send, c_recv, x_send, x_recv,
+    onward, sideways, along, across, a_send, a_recv, s_send, s_recv, b_send, b_recv, t_send, t_recv, c_send, c_recv, x_send, x_recv,
 ):
     slabs, n_pen, groups, nx, nz, at = sizes
     part = nx // GROUP
@@ -183,9 +183,16 @@
 
     steps = sorted(range(turns), key=lambda k: -min(k, turns - k))
     far_first = [(k, flips) for k in steps for flips in (1, 0) if (k, flips) != (0, 0)]
-    near = [(k, flips) for k, flips in far_first if min(k, turns - k) <= 1]
+    pair = turn + 1 - 2 * lax.rem(turn, 2)
+    fellow = (side * turns + pair) * GROUP + m
+    other_half = lax.rem(2 * turn - pair + turns, turns)
+    abreast = [
+        (lax.rem(side + flips, 2) * turns + other_half) * GROUP + mirrored(held, other_half)
+        for flips in (0, 1)
+    ]
+    beside = partner((0, 1))[1]
     members = [(g * GROUP + lax.rem(m + k, GROUP), p) for k in range(1, GROUP)]
-    others = [(partner(step)[1], p) for step in near]
+    others = [(device, p) for device in (fellow, *abreast, beside)]
     around = n_pen // 2
     ring, place = p // around, lax.rem(p, around)
 
@@ -293,8 +300,8 @@
         )
         copy.start()
         copies_a.append(copy)
-    behind = (partner((turns - 1, 0))[1], p)
-    pl.semaphore_signal(onward, inc=1, device_id=behind, device_id_type=MESH)
+    pl.semaphore_signal(onward, inc=1, device_id=(fellow, p), device_id_type=MESH)
+    pl.semaphore_signal(sideways, inc=1, device_id=(beside, p), device_id_type=MESH)
     pl.semaphore_signal(along, inc=1, device_id=(s, previous_pen), device_id_type=MESH)
     in_b[g] = jnp.zeros((part, nz), F32)
     in_t[g] = jnp.zeros((2, nz), F32)
@@ -337,6 +344,7 @@
     out_t[0] = states(at.to_later)
     out_t[1] = states(at.to_earlier)
     pl.semaphore_wait(onward, 1)
+    pl.semaphore_wait(sideways, 1)
     copies_t = to_groups(out_t, in_t, t_send, t_recv)
     own_states = states(at.local + 2 * GROUP * m)
 
@@ -542,7 +550,7 @@
             tile(nx, nz), tile(nx, nz),
             dma((6,)),
             dma, dma, dma, dma,
-            *[pltpu.SemaphoreType.REGULAR] * 3,
+            *[pltpu.SemaphoreType.REGULAR] * 4,
             dma((GROUP,)), dma((GROUP,)), dma((GROUP,)), dma((GROUP,)),
             dma((groups,)), dma((groups,)), dma((groups,)), dma((groups,)),
             dma((GROUP,)), dma((GROUP,)), dma((n_pen,)), dma((n_pen,)),

time: 33.1 us -> 32.3 us (0.976)
  Pallas kernels: 32.3 us -> 31.5 us
    pallas_call x1, Pallas kernels: 31.2 us -> 30.4 us  [per_device(): pl.pallas_call(functools.partial(kernel, (slabs, n_pen, groups, nx, nz, a...]
where the time goes in v6:
time: 32.3 us; the launch traced here: 32.2 us
  Pallas kernels  31.5 us (98%)
  between operations  0.64 us (2%)
    pallas_call x1, Pallas kernels, per_device(): pl.pallas_call(functools.partial(kernel, (slabs, n_pen, groups, nx, nz, a...  30.4 us
    pallas_call x1, Pallas kernels, per_device(): pl.pallas_call(finish, out_shape=(jax.ShapeDtypeStruct(density.shape, F32...  1.13 us

profile of v6, /device:TPU:1, one launch (start us, length us, event | category | flops | bytes accessed | tf_op | source)
XLA Modules:
  0.0 32.2 jit_solution(1108453640871047387)
XLA Ops:
  0.6 30.4 %decompose.1 = (f32[2,256,256]{2,1,0:T(8,128)S(1)}, f32[128,128]{1,0:T(8,128)S(1)}, bf16[2,256,128]{2,1,0:T(8,128)(2,1)S(1)}) custom-call(f32[2,256,256]{2,1,0:T(8,128)} %u_hbm.1, bf16[8,2,144,256]{3,2,1,0:T(8,128)(2,1)} %constant.8.clone.left_hbm, bf16[2,256,128]{2,1,0:T(8,128)(2,1)} %constant.9.clone.pz_hbm, f32[8,136,128]{2,1,0:T(8,128)} %constant.10.clone.ends_hbm, ...), custom_call_target="tpu_custom_call" | custom-call | tf_op jit(solution)/shard_map/decompose/pallas_call | solution.py:524
  31.1 1.1 %finish.1 = (f32[2,256,256]{2,1,0:T(8,128)}, f32[1,128,128]{2,1,0:T(8,128)}) custom-call(f32[2,256,256]{2,1,0:T(8,128)S(1)} %get-tuple-element.5.part, f32[128,128]{1,0:T(8,128)S(1)} %get-tuple-element.6.coarse, bf16[2,256,128]{2,1,0:T(8,128)(2,1)S(1)} %get-tuple-element.7.select), custom_call_target="tpu_custom_call" | custom-call | tf_op jit(solution)/shard_map/finish/pallas_call | solution.py:563

commit v7 on v6

--- a/solution.py
+++ b/solution.py
@@ -168,18 +168,19 @@
     turns = groups // 2
     turn, side = lax.rem(g, turns), g // turns
 
-    def mirrored(member, at_turn):
+    def turned(member, at_turn):
         there = 2 * at_turn // turns
-        return member + there * (GROUP - 2 - 2 * member + 2 * lax.rem(member, 2))
-
-    held = mirrored(m, turn)
+        half = GROUP // 2
+        return member + there * (half - GROUP * (member // half))
+
+    held = turned(m, turn)
 
     def group_at(ahead, flips):
         return lax.rem(side + flips, 2) * turns + lax.rem(turn + ahead, turns)
 
     def partner(step):
         group = group_at(*step)
-        return group, group * GROUP + mirrored(held, lax.rem(group, turns))
+        return group, group * GROUP + turned(held, lax.rem(group, turns))
 
     steps = sorted(range(turns), key=lambda k: -min(k, turns - k))
     far_first = [(k, flips) for k in steps for flips in (1, 0) if (k, flips) != (0, 0)]
@@ -187,7 +188,7 @@
     fellow = (side * turns + pair) * GROUP + m
     other_half = lax.rem(2 * turn - pair + turns, turns)
     abreast = [
-        (lax.rem(side + flips, 2) * turns + other_half) * GROUP + mirrored(held, other_half)
+        (lax.rem(side + flips, 2) * turns + other_half) * GROUP + turned(held, other_half)
         for flips in (0, 1)
     ]
     beside = partner((0, 1))[1]
@@ -294,7 +295,7 @@
     for k in range(1, GROUP):
         to = lax.rem(m + k, GROUP)
         copy = pltpu.make_async_remote_copy(
-            src_ref=out_a.at[mirrored(to, turn)], dst_ref=in_a.at[m],
+            src_ref=out_a.at[turned(to, turn)], dst_ref=in_a.at[m],
             send_sem=a_send.at[k], recv_sem=a_recv.at[k],
             device_id=(g * GROUP + to, p), device_id_type=MESH,
         )
@@ -396,21 +397,34 @@
         copy.wait_recv()
     from_earlier = weigh(at.from_earlier, 1, groups, lambda k: in_b[k])
     from_later = weigh(at.from_later, 1, groups, lambda k: in_b[k])
-    for i in range(GROUP):
-        out_c[i] = (
-            out_c[i]
-            + table[g, at.falling + i] * from_earlier
-            + table[g, at.rising + i] * from_later
-        )
-    copies_c = []
-    for k in range(1, GROUP):
-        to = lax.rem(m + k, GROUP)
+
+    def finished(row):
+        out_c[row] = (
+            out_c[row]
+            + table[g, at.falling + row] * from_earlier
+            + table[g, at.rising + row] * from_later
+        )
+
+    rank = jnp.where(m < 2, 1 - m, m)
+    copies_c, landings_c = [], []
+    for k in range(GROUP - 1):
+        nth = k + jnp.where(k >= rank, 1, 0)
+        to = jnp.where(nth < 2, 1 - nth, nth)
+        finished(to)
         copy = pltpu.make_async_remote_copy(
-            src_ref=out_c.at[to], dst_ref=in_c.at[held], send_sem=c_send.at[k], recv_sem=c_recv.at[k],
+            src_ref=out_c.at[to], dst_ref=in_c.at[held], send_sem=c_send.at[k], recv_sem=c_recv.at[m],
             device_id=(g * GROUP + to, p), device_id_type=MESH,
         )
         copy.start()
         copies_c.append(copy)
+        landings_c.append(
+            pltpu.make_async_remote_copy(
+                src_ref=out_c.at[to], dst_ref=in_c.at[turned(to, turn)],
+                send_sem=c_send.at[k], recv_sem=c_recv.at[to],
+                device_id=(g * GROUP + to, p), device_id_type=MESH,
+            )
+        )
+    finished(m)
     in_c[held] = out_c[m]
 
     fine_rows = lax.broadcasted_iota(jnp.int32, (2 * nx, nz), 0)
@@ -443,8 +457,8 @@
         x_earlier = x_earlier + pen(k) * in_x[k, 0:1, :]
         x_later = x_later + pen(n_pen + k) * in_x[k, 1:2, :]
     rest = rest + x_falling[...] * x_earlier + x_rising[...] * x_later
-    for copy in copies_c:
-        copy.wait_recv()
+    for landing in landings_c:
+        landing.wait_recv()
     coarse[...] = (in_c[...].reshape(nx, nz) + rest).T
 
 

time: 32.3 us -> 32.1 us (level)
  no operation moved by 1% of the time
where the time goes in v7:
time: 32.1 us; the launch traced here: 32 us
  Pallas kernels  31.3 us (98%)
  between operations  0.64 us (2%)
    pallas_call x1, Pallas kernels, per_device(): pl.pallas_call(functools.partial(kernel, (slabs, n_pen, groups, nx, nz, a...  30.2 us
    pallas_call x1, Pallas kernels, per_device(): pl.pallas_call(finish, out_shape=(jax.ShapeDtypeStruct(density.shape, F32...  1.13 us

profile of v7, /device:TPU:1, one launch (start us, length us, event | category | flops | bytes accessed | tf_op | source)
XLA Modules:
  0.0 32.0 jit_solution(17040059258717645351)
XLA Ops:
  0.6 30.2 %decompose.1 = (f32[2,256,256]{2,1,0:T(8,128)S(1)}, f32[128,128]{1,0:T(8,128)S(1)}, bf16[2,256,128]{2,1,0:T(8,128)(2,1)S(1)}) custom-call(f32[2,256,256]{2,1,0:T(8,128)} %u_hbm.1, bf16[8,2,144,256]{3,2,1,0:T(8,128)(2,1)} %constant.8.clone.left_hbm, bf16[2,256,128]{2,1,0:T(8,128)(2,1)} %constant.9.clone.pz_hbm, f32[8,136,128]{2,1,0:T(8,128)} %constant.10.clone.ends_hbm, ...), custom_call_target="tpu_custom_call" | custom-call | tf_op jit(solution)/shard_map/decompose/pallas_call | solution.py:538
  30.8 1.1 %finish.1 = (f32[2,256,256]{2,1,0:T(8,128)}, f32[1,128,128]{2,1,0:T(8,128)}) custom-call(f32[2,256,256]{2,1,0:T(8,128)S(1)} %get-tuple-element.5.part, f32[128,128]{1,0:T(8,128)S(1)} %get-tuple-element.6.coarse, bf16[2,256,128]{2,1,0:T(8,128)(2,1)S(1)} %get-tuple-element.7.select), custom_call_target="tpu_custom_call" | custom-call | tf_op jit(solution)/shard_map/finish/pallas_call | solution.py:577

commit v8 on v7

--- a/solution.py
+++ b/solution.py
@@ -162,8 +162,6 @@
     load_pz = pltpu.make_async_copy(pz_hbm, pz, load_sem.at[3])
     load_ends = pltpu.make_async_copy(ends_hbm.at[p], ends, load_sem.at[4])
     load_table = pltpu.make_async_copy(table_hbm, table, load_sem.at[5])
-    load_u0.start()
-    load_left.start()
 
     turns = groups // 2
     turn, side = lax.rem(g, turns), g // turns
@@ -193,7 +191,6 @@
     ]
     beside = partner((0, 1))[1]
     members = [(g * GROUP + lax.rem(m + k, GROUP), p) for k in range(1, GROUP)]
-    others = [(device, p) for device in (fellow, *abreast, beside)]
     around = n_pen // 2
     ring, place = p // around, lax.rem(p, around)
 
@@ -201,17 +198,14 @@
         return lax.rem(ring + flips, 2) * around + lax.rem(place + ahead, around)
 
     next_pen, previous_pen, across_pen = pen_at(1, 0), pen_at(around - 1, 0), pen_at(0, 1)
-    around_first = sorted(range(around), key=lambda k: -min(k, around - k))
-    far_pens = [(k, flips) for flips in (1, 0) for k in around_first if (k, flips) != (0, 0)]
     peers = [(s, q) for q in (across_pen, next_pen, previous_pen)]
-    above = (lax.rem(s + 1, slabs), p)
     below = (lax.rem(s + slabs - 1, slabs), p)
     barrier = pltpu.get_barrier_semaphore()
     for device in members:
         pl.semaphore_signal(barrier, inc=1, device_id=device, device_id_type=MESH)
-    for load in (load_u1, load_pz, load_ends, load_table):
+    for load in (load_u0, load_left, load_u1, load_pz, load_ends, load_table):
         load.start()
-    greeted = [above] + others + peers
+    greeted = peers[:1] + [(fellow, p), (beside, p)] + peers[1:] + [(device, p) for device in abreast]
     for device in greeted:
         pl.semaphore_signal(barrier, inc=1, device_id=device, device_id_type=MESH)
 
@@ -375,14 +369,21 @@
     )
     out_x[...] = own_states
     in_x[p] = own_states
-    copies_x = []
-    for k, step in enumerate(far_pens):
+    copies_x, landings_x = [], []
+    for k in range(n_pen - 1):
+        to = k + jnp.where(k >= p, 1, 0)
         copy = pltpu.make_async_remote_copy(
-            src_ref=out_x, dst_ref=in_x.at[p], send_sem=x_send.at[k], recv_sem=x_recv.at[k],
-            device_id=(s, pen_at(*step)), device_id_type=MESH,
+            src_ref=out_x, dst_ref=in_x.at[p], send_sem=x_send.at[k], recv_sem=x_recv.at[p],
+            device_id=(s, to), device_id_type=MESH,
         )
         copy.start()
         copies_x.append(copy)
+        landings_x.append(
+            pltpu.make_async_remote_copy(
+                src_ref=out_x, dst_ref=in_x.at[to], send_sem=x_send.at[k], recv_sem=x_recv.at[to],
+                device_id=(s, to), device_id_type=MESH,
+            )
+        )
 
     copy_h1.wait_recv()
     halo = jnp.where(p == n_pen - 1, c[nx - 1 : nx, :], halo_in[0:1, :])
@@ -449,8 +450,8 @@
 
     for copy in copies_s + copies_a + copies_t + copies_b + copies_x + copies_c + [copy_h1, copy_h2]:
         copy.wait_send()
-    for copy in copies_x:
-        copy.wait_recv()
+    for landing in landings_x:
+        landing.wait_recv()
     x_earlier = pen(0) * in_x[0, 0:1, :]
     x_later = pen(n_pen) * in_x[0, 1:2, :]
     for k in range(1, n_pen):

time: 32.1 us -> 32.1 us (level)
  no operation moved by 1% of the time
where the time goes in v8:
time: 32.1 us; the launch traced here: 31.9 us
  Pallas kernels  31.3 us (98%)
  between operations  0.64 us (2%)
    pallas_call x1, Pallas kernels, per_device(): pl.pallas_call(functools.partial(kernel, (slabs, n_pen, groups, nx, nz, a...  30.2 us
    pallas_call x1, Pallas kernels, per_device(): pl.pallas_call(finish, out_shape=(jax.ShapeDtypeStruct(density.shape, F32...  1.13 us

profile of v8, /device:TPU:1, one launch (start us, length us, event | category | flops | bytes accessed | tf_op | source)
XLA Modules:
  0.0 31.9 jit_solution(16124129757153437946)
XLA Ops:
  0.6 30.2 %decompose.1 = (f32[2,256,256]{2,1,0:T(8,128)S(1)}, f32[128,128]{1,0:T(8,128)S(1)}, bf16[2,256,128]{2,1,0:T(8,128)(2,1)S(1)}) custom-call(f32[2,256,256]{2,1,0:T(8,128)} %u_hbm.1, bf16[8,2,144,256]{3,2,1,0:T(8,128)(2,1)} %constant.8.clone.left_hbm, bf16[2,256,128]{2,1,0:T(8,128)(2,1)} %constant.9.clone.pz_hbm, f32[8,136,128]{2,1,0:T(8,128)} %constant.10.clone.ends_hbm, ...), custom_call_target="tpu_custom_call" | custom-call | tf_op jit(solution)/shard_map/decompose/pallas_call | solution.py:539
  30.8 1.1 %finish.1 = (f32[2,256,256]{2,1,0:T(8,128)}, f32[1,128,128]{2,1,0:T(8,128)}) custom-call(f32[2,256,256]{2,1,0:T(8,128)S(1)} %get-tuple-element.5.part, f32[128,128]{1,0:T(8,128)S(1)} %get-tuple-element.6.coarse, bf16[2,256,128]{2,1,0:T(8,128)(2,1)S(1)} %get-tuple-element.7.select), custom_call_target="tpu_custom_call" | custom-call | tf_op jit(solution)/shard_map/finish/pallas_call | solution.py:578

commit v9 on v7

--- a/solution.py
+++ b/solution.py
@@ -467,9 +467,10 @@
     coarse_out = pltpu.make_async_copy(coarse, coarse_hbm.at[0], sem.at[1])
     odd_out.start()
     coarse_out.start()
-    high, low = parts(coarse[...])
-    high, low = parts(dot(select[0], high) + dot(select[0], low))
-    even[...] = part[0] + dot(high, select[1], True) + dot(low, select[1], True)
+    along_z = jnp.concatenate([select[0], select[0]], 1)
+    along_x = jnp.concatenate([select[1], select[1]], 1)
+    spread = dot(along_z, jnp.concatenate(parts(coarse[...]), 0))
+    even[...] = part[0] + dot(jnp.concatenate(parts(spread), 1), along_x, True)
     even_out = pltpu.make_async_copy(even, fine_hbm.at[0], sem.at[2])
     even_out.start()
     odd_out.wait()

time: 32.1 us -> 32 us (level)
  no operation moved by 1% of the time
where the time goes in v9:
time: 32 us; the launch traced here: 31.9 us
  Pallas kernels  31.3 us (98%)
  between operations  0.64 us (2%)
    pallas_call x1, Pallas kernels, per_device(): pl.pallas_call(functools.partial(kernel, (slabs, n_pen, groups, nx, nz, a...  30.2 us
    pallas_call x1, Pallas kernels, per_device(): pl.pallas_call(finish, out_shape=(jax.ShapeDtypeStruct(density.shape, F32...  1.06 us

profile of v9, /device:TPU:1, one launch (start us, length us, event | category | flops | bytes accessed | tf_op | source)
XLA Modules:
  0.0 31.9 jit_solution(10631384155220367120)
XLA Ops:
  0.6 30.2 %decompose.1 = (f32[2,256,256]{2,1,0:T(8,128)S(1)}, f32[128,128]{1,0:T(8,128)S(1)}, bf16[2,256,128]{2,1,0:T(8,128)(2,1)S(1)}) custom-call(f32[2,256,256]{2,1,0:T(8,128)} %u_hbm.1, bf16[8,2,144,256]{3,2,1,0:T(8,128)(2,1)} %constant.8.clone.left_hbm, bf16[2,256,128]{2,1,0:T(8,128)(2,1)} %constant.9.clone.pz_hbm, f32[8,136,128]{2,1,0:T(8,128)} %constant.10.clone.ends_hbm, ...), custom_call_target="tpu_custom_call" | custom-call | tf_op jit(solution)/shard_map/decompose/pallas_call | solution.py:539
  30.8 1.1 %finish.1 = (f32[2,256,256]{2,1,0:T(8,128)}, f32[1,128,128]{2,1,0:T(8,128)}) custom-call(f32[2,256,256]{2,1,0:T(8,128)S(1)} %get-tuple-element.5.part, f32[128,128]{1,0:T(8,128)S(1)} %get-tuple-element.6.coarse, bf16[2,256,128]{2,1,0:T(8,128)(2,1)S(1)} %get-tuple-element.7.select), custom_call_target="tpu_custom_call" | custom-call | tf_op jit(solution)/shard_map/finish/pallas_call | solution.py:578
